TPU v7x, 32 devices: a whole 2x2x4 slice. The times are simulated.
32 devices in a mesh: rows: 4 (over y, x), cols: 8 (over z, core).
Axes of the slice: x: 2, y: 2, z: 4, core: 2. Of those that a mesh axis runs over, the one named last changes fastest.
Arguments:
- left_image: bfloat16 [32, 2048], P(('rows', 'cols')), may hold values from -8 to 8, as said below
- right_image: bfloat16 [32, 2048], P(('rows', 'cols')), may hold values from -8 to 8, as said below
- ranges: int32 [8, 2], replicated, may hold values from 0 to 63, as said below
Outputs:
- best_score: float32 [32, 2048], P('rows', 'cols')
Inputs may be any that keep to these rules, and one draw needn't show every extreme that they name: `left_image`: pixel values. `right_image`: pixel values. `ranges`: row t holds tile t's first disparity (column 0, 0 to 63) and its number of blocks of 128 disparities (column 1, 1 to 2); some tile has 2 blocks, some tile starts at 0 and some at 63.
All inputs are finite; a program needn't handle non-finite values.
Results may differ from a plain program's by a relative error of at most 0.0003.
Values may be sent and summed in bfloat16 or wider, within the bound.
No kernel may reach another device: no remote copies, remote signals or barrier semaphores. Data moves between devices by JAX's collectives and lax.ppermute only.
A program may use at most 128 MiB of HBM per device.

v0:
```python
import jax
import jax.numpy as jnp
from jax import lax
from jax.sharding import PartitionSpec as P

DB = 128
MAXB = 2
SMAX = 64


def with_halo(x, sides, width):
    for axis, dim in sides:
        peers, length = (lax.axis_size(axis), x.shape[dim])
        up = [(i, (i + 1) % peers) for i in range(peers - 1)]
        down = [(j, i) for i, j in up]
        last = lax.slice_in_dim(x, length - width, length, axis=dim)
        first = lax.slice_in_dim(x, 0, width, axis=dim)
        before = lax.ppermute(last, axis, up)
        after = lax.ppermute(first, axis, down)
        x = jnp.concatenate([before, x, after], axis=dim)
    return x


def box_sum(values, along):
    length = values.shape[along] - 6
    running = lax.slice_in_dim(values, 0, length, axis=along)
    for offset in range(1, 7):
        running = running + lax.slice_in_dim(values, offset, offset + length, axis=along)
    return running


def window_sums(values):
    return box_sum(box_sum(values, values.ndim - 1), values.ndim - 2)


def moments(pixels):
    average = window_sums(pixels) / 49.0
    spread = jnp.maximum(window_sums(pixels * pixels) / 49.0 - average * average, 0.01)
    return (average, spread)


def skewed(values, columns, lanes):
    lead = values.shape[:-1]
    length = values.shape[-1]
    tiled = jnp.broadcast_to(values[..., None, :], lead + (lanes + 1, length))
    flat = tiled.reshape(lead + ((lanes + 1) * length,))
    sheared = flat[..., : lanes * (length + 1)].reshape(lead + (lanes, length + 1))
    sheared = jnp.flip(sheared[..., :columns], axis=-2)
    return jnp.swapaxes(sheared, -1, -2)


def best_scores(left_pad, right_pad, block_count):
    height = left_pad.shape[0] - 6
    tile_width = left_pad.shape[1] - 6
    left_mean, left_spread = moments(left_pad)
    right_mean, right_spread = moments(right_pad)
    right_stats = jnp.stack([right_mean, right_spread])
    col_block = 256
    col_blocks = tile_width // col_block

    def visitor(step_index, current):
        block_id = step_index // col_blocks
        col_start = step_index % col_blocks * col_block
        source_at = col_start + 61 + DB * (MAXB - block_id) - (DB - 1)
        right_cut = lax.dynamic_slice_in_dim(right_pad, source_at, col_block + 6 + DB - 1, 1)
        right_lanes = skewed(right_cut, col_block + 6, DB)
        product = left_pad[:, :, None] * right_lanes
        cross_term = box_sum(box_sum(product, 1), 0) / 49.0
        stats_cut = lax.dynamic_slice_in_dim(right_stats, source_at, col_block + DB - 1, 2)
        stats_lanes = skewed(stats_cut, col_block, DB)
        mean_l = left_mean[:, :, None]
        spread_l = left_spread[:, :, None]
        scores = (cross_term - mean_l * stats_lanes[0]) / jnp.sqrt(spread_l * stats_lanes[1])
        best = jnp.max(scores, axis=-1)
        return jnp.maximum(current, best)

    initial = jnp.full((height, tile_width), -2.0, jnp.float32)
    return lax.fori_loop(0, block_count * col_blocks, visitor, initial)


def on_device(left_image, right_image, ranges):
    tile_count = lax.axis_size("cols")
    column_id = lax.axis_index("cols")
    strip_rows = left_image.shape[0]
    full_width = left_image.shape[1]
    tile_width = full_width // tile_count
    band_rows = strip_rows * tile_count
    window_width = tile_width + DB * (MAXB + 1)
    lead_pad = SMAX + DB * MAXB + 64
    left_tile = lax.all_to_all(
        left_image.reshape(strip_rows, tile_count, tile_width),
        "cols",
        split_axis=1,
        concat_axis=0,
        tiled=True,
    )
    left_tile = left_tile.reshape(band_rows, tile_width)
    left_pad = with_halo(left_tile, (("rows", 0), ("cols", 1)), 3)
    padded = jnp.pad(right_image, ((0, 0), (lead_pad, 64)))
    tile_ids = jnp.arange(tile_count, dtype=jnp.int32)
    window_at = tile_ids * tile_width - ranges[:, 0] + SMAX

    def cut_one(begin_at):
        return lax.dynamic_slice_in_dim(padded, begin_at, window_width, 1)

    pieces = jax.vmap(cut_one, out_axes=1)(window_at)
    received = lax.all_to_all(pieces, "cols", split_axis=1, concat_axis=0, tiled=True)
    window = received.reshape(band_rows, window_width)
    right_pad = with_halo(window, (("rows", 0),), 3)
    return best_scores(
        left_pad.astype(jnp.float32), right_pad.astype(jnp.float32), ranges[column_id, 1]
    )


def solution(mesh):
    return jax.shard_map(
        on_device,
        mesh=mesh,
        in_specs=(P(("rows", "cols"), None), P(("rows", "cols"), None), P()),
        out_specs=P("rows", "cols"),
        check_vma=False,
    )
```

profile of v0, /device:TPU:18, one launch (start us, length us, event | category | flops | bytes accessed | tf_op | source)
XLA Modules:
  0.0 179.0 jit_solution(8535279985582699032)
XLA Ops:
  2.4 5.2 %all-to-all-start = ((bf16[8,2,128]{2,1,0:T(2,128)(2,1)}), bf16[8,2,128]{2,1,0:T(2,128)(2,1)S(1)}, u32[]{:S(2)}, u32[]{:S(2)}) async-start(bf16[8,2,128]{2,1,0:T(2,128)(2,1)} %reshape.95), calls=%async_computation | async-start | bytes 8192 | tf_op jit(solution)/shard_map/all_to_all | solution.py:90
  9.0 10.7 %while.17 = (s32[]{:T(128)}, bf16[1,2496]{1,0:T(2,128)(2,1)S(1)}, s32[8,2]{0,1:T(2,128)S(1)}, bf16[8,1,640]{2,1,0:T(2,128)(2,1)S(1)}, s32[]{:T(128)}) while((s32[]{:T(128)}, bf16[1,2496]{1,0:T(2,128)(2,1)S(1)}, s32[8,2]{0,1:T(2,128)S(1)}, bf16[8,1,640]{2,1,0:T(2,128)(2,1)S(1)}, s32[]{:T(128)}) %tuple.57), condition=%wide.while_cond, body=%wide.while_body.sunk | while | flops 2 | bytes 5217 | solution.py:104
  19.8 3.4 %collective-permute-start = (bf16[3,256]{1,0:T(4,128)(2,1)S(1)}, bf16[3,256]{1,0:T(4,128)(2,1)S(1)}, u32[]{:S(2)}, u32[]{:S(2)}) collective-permute-start(bf16[3,256]{1,0:T(4,128)(2,1)S(1)} %slice_bitcast_fusion.3), channel_id=1, source_target_pairs={{0,8},{8,16},{16,24},{1,9},{9,17},{17,25},{2,10},{10,18},{18,26},{... | collective-permute-start | bytes 4616 | tf_op jit(solution)/shard_map/ppermute | solution.py:18
  23.2 2.4 %collective-permute-start.1 = (bf16[3,256]{1,0:T(4,128)(2,1)S(1)}, bf16[3,256]{1,0:T(4,128)(2,1)S(1)}, u32[]{:S(2)}, u32[]{:S(2)}) collective-permute-start(bf16[3,256]{1,0:T(4,128)(2,1)S(1)} %bitcast.94), channel_id=1, source_target_pairs={{8,0},{16,8},{24,16},{9,1},{17,9},{25,17},{10,2},{18,10},{26,18},{... | collective-permute-start | bytes 4616 | tf_op jit(solution)/shard_map/ppermute | solution.py:19
  27.0 5.1 %all-to-all-start.1 = ((bf16[8,2,320]{2,1,0:T(2,128)(2,1)}), bf16[8,2,320]{2,1,0:T(2,128)(2,1)S(1)}, u32[]{:S(2)}, u32[]{:S(2)}) async-start(bf16[8,2,320]{2,1,0:T(2,128)(2,1)} %reshape.97), calls=%async_computation.1 | async-start | bytes 24576 | tf_op jit(solution)/shard_map/all_to_all | solution.py:107
  33.5 2.0 %collective-permute-start.2 = (bf16[14,3]{1,0:T(8,128)(2,1)S(1)}, bf16[14,3]{1,0:T(8,128)(2,1)S(1)}, u32[]{:S(2)}, u32[]{:S(2)}) collective-permute-start(bf16[14,3]{1,0:T(8,128)(2,1)S(1)} %get-tuple-element.241), channel_id=1, source_target_pairs={{0,1},{1,2},{2,3},{3,4},{4,5},{5,6},{6,7},{8,9},{9,10},{10,11},{11... | collective-permute-start | bytes 260 | tf_op jit(solution)/shard_map/ppermute | solution.py:18
  35.5 3.5 %collective-permute-start.3 = (bf16[14,3]{1,0:T(8,128)(2,1)S(1)}, bf16[14,3]{1,0:T(8,128)(2,1)S(1)}, u32[]{:S(2)}, u32[]{:S(2)}) collective-permute-start(bf16[14,3]{1,0:T(8,128)(2,1)S(1)} %get-tuple-element.242), channel_id=1, source_target_pairs={{1,0},{2,1},{3,2},{4,3},{5,4},{6,5},{7,6},{9,8},{10,9},{11,10},{12... | collective-permute-start | bytes 260 | tf_op jit(solution)/shard_map/ppermute | solution.py:19
  40.8 4.3 %collective-permute-start.4 = (bf16[3,640]{1,0:T(4,128)(2,1)S(1)}, bf16[3,640]{1,0:T(4,128)(2,1)S(1)}, u32[]{:S(2)}, u32[]{:S(2)}) collective-permute-start(bf16[3,640]{1,0:T(4,128)(2,1)S(1)} %slice_bitcast_fusion.2), channel_id=1, source_target_pairs={{0,8},{8,16},{16,24},{1,9},{9,17},{17,25},{2,10},{10,18},{18,26},{... | collective-permute-start | bytes 11528 | tf_op jit(solution)/shard_map/ppermute | solution.py:18
  45.1 1.9 %collective-permute-start.5 = (bf16[3,640]{1,0:T(4,128)(2,1)S(1)}, bf16[3,640]{1,0:T(4,128)(2,1)S(1)}, u32[]{:S(2)}, u32[]{:S(2)}) collective-permute-start(bf16[3,640]{1,0:T(4,128)(2,1)S(1)} %bitcast.93), channel_id=1, source_target_pairs={{8,0},{16,8},{24,16},{9,1},{17,9},{25,17},{10,2},{18,10},{26,18},{... | collective-permute-start | bytes 11528 | tf_op jit(solution)/shard_map/ppermute | solution.py:19
  47.1 4.4 %collective-permute-done.5 = bf16[3,640]{1,0:T(4,128)(2,1)S(1)} collective-permute-done((bf16[3,640]{1,0:T(4,128)(2,1)S(1)}, bf16[3,640]{1,0:T(4,128)(2,1)S(1)}, u32[]{:S(2)}, u32[]{:S(2)}) %collective-permute-start.5) | collective-permute-done | bytes 3872 | tf_op jit(solution)/shard_map/ppermute | solution.py:19
  51.8 126.6 %while.16 = (s32[]{:T(128)}, f32[8,256]{1,0:T(8,128)S(1)}, s32[]{:T(128)}, f32[14,262]{1,0:T(8,128)S(1)}, f32[14,640]{1,0:T(8,128)S(1)}, /*index=5*/f32[8,256]{1...) while((s32[]{:T(128)}, f32[8,256]{1,0:T(8,128)S(1)}, ...), condition=%wide.region_2.3_spmd, body=%wide.region_0.2_spmd.sunk | while | flops 6367754 | bytes 92431232 | solution.py:78
  52.6 2.4 %broadcast_in_dim.37 = f32[14,129,389]{2,1,0:T(8,128)} broadcast(f32[14,389]{1,0:T(8,128)S(1)} %constant_dynamic-slice_fusion.8), dimensions={0,2} | broadcast | bytes 2831920 | tf_op jit(solution)/shard_map/while/body/broadcast_in_dim | solution.py:45
  54.9 3.7 %reshape.103 = f32[14,50181]{1,0:T(8,128)S(1)} reshape(f32[14,129,389]{2,1,0:T(8,128)} %broadcast_in_dim.37) | data formatting | bytes 5620272 | tf_op jit(solution)/shard_map/while/body/reshape | solution.py:46
  58.6 1.9 %slice.827 = f32[14,49920]{1,0:T(8,128)} slice(f32[14,50181]{1,0:T(8,128)S(1)} %reshape.103), slice={[0:14], [0:49920]} | slice | bytes 5591040 | tf_op jit(solution)/shard_map/while/body/slice | solution.py:47
  60.5 5.9 %reshape.104 = f32[14,128,390]{2,1,0:T(8,128)} reshape(f32[14,49920]{1,0:T(8,128)} %slice.827) | data formatting | bytes 5591040 | tf_op jit(solution)/shard_map/while/body/reshape | solution.py:47
  68.2 13.5 %rev.25 = f32[14,128,262]{2,1,0:T(8,128)} reverse(f32[14,128,262]{2,1,0:T(8,128)S(1)} %slice-done.1), dimensions={1} | reverse | bytes 3756032 | tf_op jit(solution)/shard_map/while/body/jit(_flip)/rev | solution.py:48
  81.6 2.0 %multiply_bitcast_fusion.2 = f32[14,262,128]{1,2,0:T(8,128)S(1)} fusion(f32[14,128,262]{2,1,0:T(8,128)} %rev.25, f32[14,262]{1,0:T(8,128)S(1)} %get-tuple-element.372), kind=kLoop, calls=%fused_computation.1.clone.1 | loop fusion | flops 469504 | bytes 3770704 | tf_op jit(solution)/shard_map/while/body/mul | solution.py:67
  83.7 2.9 %slice_add_fusion.61 = f32[14,256,128]{1,2,0:T(8,128)S(1)} fusion(f32[14,262,128]{1,2,0:T(8,128)S(1)} %multiply_bitcast_fusion.2), kind=kLoop, calls=%fused_computation.2.clone.1 | loop fusion | flops 2752512 | bytes 14680064 | tf_op jit(solution)/shard_map/while/body/add | solution.py:28
  86.6 1.9 %broadcast_in_dim.36 = f32[2,8,129,383]{3,2,1,0:T(8,128)} broadcast(f32[2,8,383]{2,1,0:T(8,128)S(1)} %constant_dynamic-slice_fusion.7), dimensions={0,1,3} | broadcast | bytes 3186560 | tf_op jit(solution)/shard_map/while/body/broadcast_in_dim | solution.py:45
  88.6 3.6 %reshape.102 = f32[2,8,49407]{2,1,0:T(8,128)} reshape(f32[2,8,129,383]{3,2,1,0:T(8,128)} %broadcast_in_dim.36) | data formatting | bytes 6324096 | tf_op jit(solution)/shard_map/while/body/reshape | solution.py:46
  96.2 16.6 %rev.24 = f32[2,8,128,256]{3,2,1,0:T(8,128)} reverse(f32[2,8,128,256]{3,2,1,0:T(8,128)} %slice.826), dimensions={2} | reverse | bytes 4194304 | tf_op jit(solution)/shard_map/while/body/jit(_flip)/rev | solution.py:48
  112.8 2.0 %fusion.22 = f32[8,256]{1,0:T(8,128)S(1)} fusion(f32[2,8,256,128]{2,3,1,0:T(8,128)} %bitcast.79, f32[14,256,128]{1,2,0:T(8,128)S(1)} %slice_add_fusion.61, f32[8,256]{1,0:T(8,128)S(1)} %get-tuple-element.376, f32[8,256]{1,0:T(8,128)S(1)} %get-tuple-element.374), kind=kLoop, calls=%fused_computation.12.clone.1 | loop fusion | flops 3143680 | bytes 9461760 | tf_op jit(solution)/shard_map/while/body/reduce_max | solution.py:74
  115.5 2.4 %broadcast_in_dim.37 = f32[14,129,389]{2,1,0:T(8,128)} broadcast(f32[14,389]{1,0:T(8,128)S(1)} %constant_dynamic-slice_fusion.8), dimensions={0,2} | broadcast | bytes 2831920 | tf_op jit(solution)/shard_map/while/body/broadcast_in_dim | solution.py:45
  117.9 3.7 %reshape.103 = f32[14,50181]{1,0:T(8,128)S(1)} reshape(f32[14,129,389]{2,1,0:T(8,128)} %broadcast_in_dim.37) | data formatting | bytes 5620272 | tf_op jit(solution)/shard_map/while/body/reshape | solution.py:46
  123.5 5.9 %reshape.104 = f32[14,128,390]{2,1,0:T(8,128)} reshape(f32[14,49920]{1,0:T(8,128)} %slice.827) | data formatting | bytes 5591040 | tf_op jit(solution)/shard_map/while/body/reshape | solution.py:47
  131.2 13.5 %rev.25 = f32[14,128,262]{2,1,0:T(8,128)} reverse(f32[14,128,262]{2,1,0:T(8,128)S(1)} %slice-done.1), dimensions={1} | reverse | bytes 3756032 | tf_op jit(solution)/shard_map/while/body/jit(_flip)/rev | solution.py:48
  144.6 2.0 %multiply_bitcast_fusion.2 = f32[14,262,128]{1,2,0:T(8,128)S(1)} fusion(f32[14,128,262]{2,1,0:T(8,128)} %rev.25, f32[14,262]{1,0:T(8,128)S(1)} %get-tuple-element.372), kind=kLoop, calls=%fused_computation.1.clone.1 | loop fusion | flops 469504 | bytes 3770704 | tf_op jit(solution)/shard_map/while/body/mul | solution.py:67
  146.6 2.9 %slice_add_fusion.61 = f32[14,256,128]{1,2,0:T(8,128)S(1)} fusion(f32[14,262,128]{1,2,0:T(8,128)S(1)} %multiply_bitcast_fusion.2), kind=kLoop, calls=%fused_computation.2.clone.1 | loop fusion | flops 2752512 | bytes 14680064 | tf_op jit(solution)/shard_map/while/body/add | solution.py:28
  149.6 1.9 %broadcast_in_dim.36 = f32[2,8,129,383]{3,2,1,0:T(8,128)} broadcast(f32[2,8,383]{2,1,0:T(8,128)S(1)} %constant_dynamic-slice_fusion.7), dimensions={0,1,3} | broadcast | bytes 3186560 | tf_op jit(solution)/shard_map/while/body/broadcast_in_dim | solution.py:45
  151.5 3.6 %reshape.102 = f32[2,8,49407]{2,1,0:T(8,128)} reshape(f32[2,8,129,383]{3,2,1,0:T(8,128)} %broadcast_in_dim.36) | data formatting | bytes 6324096 | tf_op jit(solution)/shard_map/while/body/reshape | solution.py:46
  159.2 16.6 %rev.24 = f32[2,8,128,256]{3,2,1,0:T(8,128)} reverse(f32[2,8,128,256]{3,2,1,0:T(8,128)} %slice.826), dimensions={2} | reverse | bytes 4194304 | tf_op jit(solution)/shard_map/while/body/jit(_flip)/rev | solution.py:48
  175.8 2.0 %fusion.22 = f32[8,256]{1,0:T(8,128)S(1)} fusion(f32[2,8,256,128]{2,3,1,0:T(8,128)} %bitcast.79, f32[14,256,128]{1,2,0:T(8,128)S(1)} %slice_add_fusion.61, f32[8,256]{1,0:T(8,128)S(1)} %get-tuple-element.376, f32[8,256]{1,0:T(8,128)S(1)} %get-tuple-element.374), kind=kLoop, calls=%fused_computation.12.clone.1 | loop fusion | flops 3143680 | bytes 9461760 | tf_op jit(solution)/shard_map/while/body/reduce_max | solution.py:74
  (85 shorter events, 33.6 us)
Async XLA Ops:
  2.4 17.3 %all-to-all-start = ((bf16[8,2,128]{2,1,0:T(2,128)(2,1)}), bf16[8,2,128]{2,1,0:T(2,128)(2,1)S(1)}, u32[]{:S(2)}, u32[]{:S(2)}) async-start(bf16[8,2,128]{2,1,0:T(2,128)(2,1)} %reshape.95), calls=%async_computation | async-start | bytes 8192 | tf_op jit(solution)/shard_map/all_to_all | solution.py:90
  19.8 13.6 %collective-permute-start = (bf16[3,256]{1,0:T(4,128)(2,1)S(1)}, bf16[3,256]{1,0:T(4,128)(2,1)S(1)}, u32[]{:S(2)}, u32[]{:S(2)}) collective-permute-start(bf16[3,256]{1,0:T(4,128)(2,1)S(1)} %slice_bitcast_fusion.3), channel_id=1, source_target_pairs={{0,8},{8,16},{16,24},{1,9},{9,17},{17,25},{2,10},{10,18},{18,26},{... | collective-permute-start | bytes 4616 | tf_op jit(solution)/shard_map/ppermute | solution.py:18
  23.2 10.2 %collective-permute-start.1 = (bf16[3,256]{1,0:T(4,128)(2,1)S(1)}, bf16[3,256]{1,0:T(4,128)(2,1)S(1)}, u32[]{:S(2)}, u32[]{:S(2)}) collective-permute-start(bf16[3,256]{1,0:T(4,128)(2,1)S(1)} %bitcast.94), channel_id=1, source_target_pairs={{8,0},{16,8},{24,16},{9,1},{17,9},{25,17},{10,2},{18,10},{26,18},{... | collective-permute-start | bytes 4616 | tf_op jit(solution)/shard_map/ppermute | solution.py:19
  27.0 13.7 %all-to-all-start.1 = ((bf16[8,2,320]{2,1,0:T(2,128)(2,1)}), bf16[8,2,320]{2,1,0:T(2,128)(2,1)S(1)}, u32[]{:S(2)}, u32[]{:S(2)}) async-start(bf16[8,2,320]{2,1,0:T(2,128)(2,1)} %reshape.97), calls=%async_computation.1 | async-start | bytes 24576 | tf_op jit(solution)/shard_map/all_to_all | solution.py:107
  33.5 5.6 %collective-permute-start.2 = (bf16[14,3]{1,0:T(8,128)(2,1)S(1)}, bf16[14,3]{1,0:T(8,128)(2,1)S(1)}, u32[]{:S(2)}, u32[]{:S(2)}) collective-permute-start(bf16[14,3]{1,0:T(8,128)(2,1)S(1)} %get-tuple-element.241), channel_id=1, source_target_pairs={{0,1},{1,2},{2,3},{3,4},{4,5},{5,6},{6,7},{8,9},{9,10},{10,11},{11... | collective-permute-start | bytes 260 | tf_op jit(solution)/shard_map/ppermute | solution.py:18
  35.5 4.8 %collective-permute-start.3 = (bf16[14,3]{1,0:T(8,128)(2,1)S(1)}, bf16[14,3]{1,0:T(8,128)(2,1)S(1)}, u32[]{:S(2)}, u32[]{:S(2)}) collective-permute-start(bf16[14,3]{1,0:T(8,128)(2,1)S(1)} %get-tuple-element.242), channel_id=1, source_target_pairs={{1,0},{2,1},{3,2},{4,3},{5,4},{6,5},{7,6},{9,8},{10,9},{11,10},{12... | collective-permute-start | bytes 260 | tf_op jit(solution)/shard_map/ppermute | solution.py:19
  40.8 6.3 %collective-permute-start.4 = (bf16[3,640]{1,0:T(4,128)(2,1)S(1)}, bf16[3,640]{1,0:T(4,128)(2,1)S(1)}, u32[]{:S(2)}, u32[]{:S(2)}) collective-permute-start(bf16[3,640]{1,0:T(4,128)(2,1)S(1)} %slice_bitcast_fusion.2), channel_id=1, source_target_pairs={{0,8},{8,16},{16,24},{1,9},{9,17},{17,25},{2,10},{10,18},{18,26},{... | collective-permute-start | bytes 11528 | tf_op jit(solution)/shard_map/ppermute | solution.py:18
  45.1 6.4 %collective-permute-start.5 = (bf16[3,640]{1,0:T(4,128)(2,1)S(1)}, bf16[3,640]{1,0:T(4,128)(2,1)S(1)}, u32[]{:S(2)}, u32[]{:S(2)}) collective-permute-start(bf16[3,640]{1,0:T(4,128)(2,1)S(1)} %bitcast.93), channel_id=1, source_target_pairs={{8,0},{16,8},{24,16},{9,1},{17,9},{25,17},{10,2},{18,10},{26,18},{... | collective-permute-start | bytes 11528 | tf_op jit(solution)/shard_map/ppermute | solution.py:19
  66.4 1.8 slice-start.1
  92.2 1.9 %slice-start = ((f32[2,8,49407]{2,1,0:T(8,128)}), f32[2,8,49152]{2,1,0:T(8,128)S(1)}, s32[]{:S(2)}) async-start(f32[2,8,49407]{2,1,0:T(8,128)} %reshape.102), calls=%async_computation.2 | async-start | bytes 6291456 | tf_op jit(solution)/shard_map/while/body/slice | solution.py:47
  129.4 1.8 slice-start.1
  155.2 1.9 %slice-start = ((f32[2,8,49407]{2,1,0:T(8,128)}), f32[2,8,49152]{2,1,0:T(8,128)S(1)}, s32[]{:S(2)}) async-start(f32[2,8,49407]{2,1,0:T(8,128)} %reshape.102), calls=%async_computation.2 | async-start | bytes 6291456 | tf_op jit(solution)/shard_map/while/body/slice | solution.py:47
  178.4 0.6 copy-start
where the time goes:
time: 182 us; the launch traced here: 179 us
  local copies, waits for them, and re-layouts  126 us (69%)
  starting transfers between devices  27.9 us (15%)
  other arithmetic  17 us (9%)
  waiting for transfers between devices  5.76 us (3%)
  loops' own time  1.99 us (1%)
    rev x4, local copies, waits for them, and re-layouts, skewed(): sheared = jnp.flip(sheared[..., :columns], axis=-2)  60.1 us
    reshape x4, local copies, waits for them, and re-layouts, skewed(): flat = tiled.reshape(lead + ((lanes + 1) * length,))  14.6 us
    reshape x2, local copies, waits for them, and re-layouts, skewed(): flat[..., :lanes * (length + 1)].reshape(lead + (lanes, length + 1))  11.8 us
    gather x24, local copies, waits for them, and re-layouts  10.7 us
    ppermute x3, starting transfers between devices, with_halo(): before = lax.ppermute(last, axis, up)  9.75 us
    broadcast_in_dim x4, local copies, waits for them, and re-layouts, skewed(): tiled = jnp.broadcast_to(values[..., None, :], lead + (lanes + 1, length))  8.52 us
    ppermute x3, starting transfers between devices, with_halo(): after = lax.ppermute(first, axis, down)  7.86 us
    slice x6, local copies, waits for them, and re-layouts, skewed(): flat[..., :lanes * (length + 1)].reshape(lead + (lanes, length + 1))  7.57 us
  transfers between devices with their start and end apart: 8, of which 2 were waited for; matrix products, arithmetic and copies ran while one was open for 8% of the time, Pallas kernels for 0%

commit v1 on v0

v1 whole, which is shorter than its diff:
```python
import functools

import jax
import jax.numpy as jnp
from jax import lax
from jax.experimental import pallas as pl
from jax.experimental.pallas import tpu as pltpu
from jax.sharding import PartitionSpec as P

DB = 128
MAXB = 2
LANES = 128
LEFT_TILES = 3
RIGHT_TILES = 5
TILES = LEFT_TILES + RIGHT_TILES
LEAD = 3
GROUP = 8
FAR = 3.0e37
VMEM = pl.BlockSpec(memory_space=pltpu.VMEM)
SMEM = pl.BlockSpec(memory_space=pltpu.SMEM)


def pack_kernel(bands, tiles, left_ref, right_ref, ranges_ref, out_ref, low_ref, left_rows, right_rows):
    strip, width = left_ref.shape
    per_tile = width // tiles // LANES
    lane = lax.broadcasted_iota(jnp.int32, (8, LANES), 1)
    low = MAXB * DB - DB * ranges_ref[lax.axis_index("cols"), 1]
    low_ref[...] = jnp.full(low_ref.shape, low, jnp.int32)
    left_rows[...] = jnp.zeros_like(left_rows)
    right_rows[...] = jnp.zeros_like(right_rows)
    for line in range(strip):
        for chunk in range(width // LANES):
            cut = slice(chunk * LANES, (chunk + 1) * LANES)
            left_rows[LEAD + chunk : LEAD + chunk + 1, :] = left_ref[line : line + 1, cut].astype(jnp.float32)
            right_rows[LEAD + chunk : LEAD + chunk + 1, :] = right_ref[line : line + 1, cut].astype(jnp.float32)

        def shifted(rows, begin):
            first = begin // LANES
            offset = begin - first * LANES
            here = pltpu.roll(rows[pl.ds(first, 8), :], LANES - offset, 1)
            after = pltpu.roll(rows[pl.ds(first + 1, 8), :], LANES - offset, 1)
            return jnp.where(lane < LANES - offset, here, after)

        for tile in range(tiles):
            base = (LEAD + tile * per_tile) * LANES
            left_part = shifted(left_rows, base - 3)[:LEFT_TILES]
            right_part = shifted(right_rows, base - 3 - (MAXB * DB - 1) - ranges_ref[tile, 0])[:RIGHT_TILES]
            piece = jnp.concatenate([left_part, right_part], 0).astype(jnp.bfloat16)
            for band in range(bands):
                out_ref[band * tiles + tile, line] = piece


def pack(left, right, ranges, bands, tiles):
    strip, width = left.shape
    rows = LEAD + width // LANES + 13
    return pl.pallas_call(
        functools.partial(pack_kernel, bands, tiles),
        out_shape=[
            jax.ShapeDtypeStruct((bands * tiles, strip, TILES, LANES), jnp.bfloat16),
            jax.ShapeDtypeStruct((8, LANES), jnp.int32),
        ],
        in_specs=[VMEM, VMEM, SMEM],
        out_specs=[VMEM, VMEM],
        scratch_shapes=[pltpu.VMEM((rows, LANES), jnp.float32), pltpu.VMEM((rows, LANES), jnp.float32)],
        compiler_params=pltpu.CompilerParams(vmem_limit_bytes=8 * 2**20),
    )(left, right, ranges)


def ahead(values, by, axis):
    return pltpu.roll(values, values.shape[axis] - by, axis)


def box(values, axis):
    two = values + ahead(values, 1, axis)
    four = two + ahead(two, 2, axis)
    return four + ahead(two, 4, axis) + ahead(values, 6, axis)


def moments(pixels):
    total = box(box(pixels, 1), 0)[:GROUP]
    mean = total / 49.0
    spread = jnp.maximum(box(box(pixels * pixels, 1), 0)[:GROUP] / 49.0 - mean * mean, 0.01)
    return total, mean, spread


def parts(values):
    high = values.astype(jnp.bfloat16)
    rest = values - high.astype(jnp.float32)
    middle = rest.astype(jnp.bfloat16)
    low = (rest - middle.astype(jnp.float32)).astype(jnp.bfloat16)
    return [p.astype(jnp.float32) for p in (high, middle, low)]


def score_kernel(height, lines_ref, low_ref, out_ref, rows):
    band_rows, tile_width = out_ref.shape
    row = lax.broadcasted_iota(jnp.int32, (16, 1), 0)
    row8 = lax.broadcasted_iota(jnp.int32, (GROUP, 1), 0)
    span = MAXB * DB + LANES
    past = lax.broadcasted_iota(jnp.int32, (span, LANES), 0) - lax.broadcasted_iota(jnp.int32, (span, LANES), 1)
    inside = (past >= low_ref[0:1, :]) & (past < MAXB * DB)
    cap = jnp.where(inside, FAR, -FAR)
    rows[...] = jnp.zeros_like(rows)
    for group in range(band_rows // GROUP):
        first = lax.axis_index("rows") * band_rows + group * GROUP - 3
        for i in range(GROUP + 6):
            y = first + i
            valid = ((y >= 0) & (y < height)).astype(jnp.float32)
            line = lines_ref[jnp.clip(y, 0, height - 1)].astype(jnp.float32)
            rows[i * TILES : (i + 1) * TILES, :] = line * valid
        tiles = [rows[pl.ds(t, 16, stride=TILES), :] for t in range(TILES)]
        left = jnp.concatenate(tiles[:LEFT_TILES], 1)
        right = jnp.concatenate(tiles[LEFT_TILES:], 1)
        left_total, _, left_spread = moments(left)
        _, right_mean, right_spread = moments(right)
        reach = tile_width + MAXB * DB
        left_scale = lax.rsqrt(left_spread[:, :tile_width]) * (1.0 / 49.0)
        right_scale = jnp.transpose(lax.rsqrt(right_spread[:, :reach]))
        left_parts = parts(-left_total[:, :tile_width])
        right_parts = parts(right_mean[:, :reach])
        shifted_left = [(left if j == 0 else ahead(left, j, 1))[:, :tile_width] for j in range(7)]
        shifted_right = [(right if j == 0 else ahead(right, j, 1))[:, :reach] for j in range(7)]
        right_side = jnp.concatenate(shifted_right + [b for _ in range(3) for b in right_parts], 0)
        right_side = jnp.transpose(right_side).astype(jnp.bfloat16)
        result = []
        for y in range(GROUP):
            window = ((row >= y) & (row < y + 7)).astype(jnp.float32)
            only = (row8 == y).astype(jnp.float32)
            left_side = [v * window for v in shifted_left] + [a * only for a in left_parts for _ in range(3)]
            left_side = jnp.concatenate(left_side, 0).astype(jnp.bfloat16)
            halves = []
            for block in range(tile_width // LANES):
                at = block * LANES
                products = jnp.dot(
                    right_side[at : at + span],
                    left_side[:, at : at + LANES],
                    preferred_element_type=jnp.float32,
                )
                scaled = products * right_scale[at : at + span, y : y + 1]
                halves.append(jnp.max(jnp.minimum(scaled, cap), axis=0, keepdims=True))
            result.append(jnp.concatenate(halves, 1))
        best = jnp.concatenate(result, 0) * left_scale
        out_ref[group * GROUP : (group + 1) * GROUP, :] = jnp.maximum(best, -2.0)


def score(lines, low, band_rows, tile_width):
    return pl.pallas_call(
        functools.partial(score_kernel, lines.shape[0]),
        out_shape=jax.ShapeDtypeStruct((band_rows, tile_width), jnp.float32),
        in_specs=[VMEM, VMEM],
        out_specs=VMEM,
        scratch_shapes=[pltpu.VMEM((16 * TILES, LANES), jnp.float32)],
        compiler_params=pltpu.CompilerParams(vmem_limit_bytes=16 * 2**20),
    )(lines, low)


def on_device(left_image, right_image, ranges):
    bands, tiles = lax.axis_size("rows"), lax.axis_size("cols")
    strip, width = left_image.shape
    pieces, low = pack(left_image, right_image, ranges, bands, tiles)
    lines = lax.all_to_all(pieces, ("rows", "cols"), split_axis=0, concat_axis=0, tiled=True)
    lines = lines.reshape(bands * tiles * strip, TILES, LANES)
    return score(lines, low, strip * tiles, width // tiles)


def solution(mesh):
    return jax.shard_map(
        on_device,
        mesh=mesh,
        in_specs=(P(("rows", "cols"), None), P(("rows", "cols"), None), P()),
        out_specs=P("rows", "cols"),
        check_vma=False,
    )
```

time: 182 us -> 19.8 us (0.11)
  the two profiles are of different devices: /device:TPU:18 before, /device:TPU:0 now
where the time goes in v1:
time: 19.8 us; the launch traced here: 19.5 us
  blocking collectives  14.5 us (73%)
  Pallas kernels  2.89 us (15%)
  local copies, waits for them, and re-layouts  2.15 us (11%)
    all_to_all x1, blocking collectives, on_device(): lax.all_to_all(pieces, ('rows', 'cols'), split_axis=0, concat_axis=0, til...  14.5 us
    pallas_call x1, Pallas kernels, score(): pl.pallas_call(functools.partial(score_kernel, lines.shape[0]), out_shape...  2.15 us
    unnamed x5, local copies, waits for them, and re-layouts  2.15 us
    pallas_call x1, Pallas kernels, pack(): pl.pallas_call(functools.partial(pack_kernel, bands, tiles), out_shape=[j...  0.74 us

profile of v1, /device:TPU:0, one launch (start us, length us, event | category | flops | bytes accessed | tf_op | source)
XLA Modules:
  0.0 19.5 jit_solution(13998892444920661203)
XLA Ops:
  0.0 0.8 %copy.6.ranges_ref = s32[8,2]{1,0:T(8,128)S(1)} copy(s32[8,2]{0,1:T(2,128)} %param.5) | data formatting | bytes 128 | tf_op args[2]
  0.8 0.0 copy-start
  0.8 0.7 %copy-done = bf16[1,2048]{1,0:T(2,128)(2,1)S(1)} copy-done((bf16[1,2048]{1,0:T(2,128)(2,1)S(1)}, bf16[1,2048]{1,0:T(2,128)(2,1)}, u32[]{:S(2)}) %copy-start) | copy-done | bytes 4120
  1.5 0.0 copy-start.1
  1.5 0.7 %copy-done.1 = bf16[1,2048]{1,0:T(2,128)(2,1)S(1)} copy-done((bf16[1,2048]{1,0:T(2,128)(2,1)S(1)}, bf16[1,2048]{1,0:T(2,128)(2,1)}, u32[]{:S(2)}) %copy-start.1) | copy-done | bytes 4120
  2.1 0.7 %shard_map.37 = (bf16[32,1,8,128]{3,2,1,0:T(8,128)(2,1)S(1)}, s32[8,128]{1,0:T(8,128)S(1)}) custom-call(bf16[1,2048]{1,0:T(2,128)(2,1)S(1)} %copy-done, bf16[1,2048]{1,0:T(2,128)(2,1)S(1)} %copy-done.1, s32[8,2]{1,0:T(8,128)S(1)} %copy.6.ranges_ref), custom_call_target="tpu_custom_call" | custom-call | tf_op jit(solution)/shard_map/pallas_call | solution.py:56
  2.9 14.5 %all_to_all.5 = bf16[32,1,8,128]{3,2,1,0:T(8,128)(2,1)S(1)} all-to-all(bf16[32,1,8,128]{3,2,1,0:T(8,128)(2,1)S(1)} %get-tuple-element.7), channel_id=1, replica_groups=mesh['rows'=4,'cols'=8] {'rows','cols'}, dimensions={0} | all-to-all | bytes 131072 | tf_op jit(solution)/shard_map/all_to_all | solution.py:160
  17.4 2.2 %shard_map.38 = f32[8,256]{1,0:T(8,128)} custom-call(bf16[32,8,128]{2,1,0:T(8,128)(2,1)S(1)} %bitcast.1, s32[8,128]{1,0:T(8,128)S(1)} %get-tuple-element.8.low_ref), custom_call_target="tpu_custom_call" | custom-call | tf_op jit(solution)/shard_map/pallas_call | solution.py:146
Async XLA Ops:
  0.8 0.7 %copy-start = (bf16[1,2048]{1,0:T(2,128)(2,1)S(1)}, bf16[1,2048]{1,0:T(2,128)(2,1)}, u32[]{:S(2)}) copy-start(bf16[1,2048]{1,0:T(2,128)(2,1)} %left_ref.1) | copy-start | bytes 12292
  1.5 0.7 %copy-start.1 = (bf16[1,2048]{1,0:T(2,128)(2,1)S(1)}, bf16[1,2048]{1,0:T(2,128)(2,1)}, u32[]{:S(2)}) copy-start(bf16[1,2048]{1,0:T(2,128)(2,1)} %right_ref.1) | copy-start | bytes 12292

commit v2 on v1

--- a/solution.py
+++ b/solution.py
@@ -17,34 +17,44 @@
 GROUP = 8
 FAR = 3.0e37
 VMEM = pl.BlockSpec(memory_space=pltpu.VMEM)
-SMEM = pl.BlockSpec(memory_space=pltpu.SMEM)
+HBM = pl.BlockSpec(memory_space=pltpu.HBM)
 
 
-def pack_kernel(bands, tiles, left_ref, right_ref, ranges_ref, out_ref, low_ref, left_rows, right_rows):
+def pack_kernel(bands, tiles, left_hbm, right_hbm, ranges_hbm, out_ref, low_ref, left_ref, right_ref, ranges_ref, left_rows, right_rows, sems):
+    copies = [
+        pltpu.make_async_copy(source, target, sems.at[i])
+        for i, (source, target) in enumerate(
+            [(ranges_hbm, ranges_ref), (left_hbm, left_ref), (right_hbm, right_ref)]
+        )
+    ]
+    for copy in copies:
+        copy.start()
     strip, width = left_ref.shape
-    per_tile = width // tiles // LANES
+    chunks = width // LANES
+    per_tile = chunks // tiles
     lane = lax.broadcasted_iota(jnp.int32, (8, LANES), 1)
-    low = MAXB * DB - DB * ranges_ref[lax.axis_index("cols"), 1]
-    low_ref[...] = jnp.full(low_ref.shape, low, jnp.int32)
     left_rows[...] = jnp.zeros_like(left_rows)
     right_rows[...] = jnp.zeros_like(right_rows)
+    for copy in copies:
+        copy.wait()
+    low = MAXB * DB - DB * ranges_ref[1, lax.axis_index("cols")]
+    low_ref[...] = jnp.full(low_ref.shape, low, jnp.int32)
+
+    def shifted(rows, first, by):
+        here = pltpu.roll(rows[first : first + 8, :], by, 1)
+        after = pltpu.roll(rows[first + 1 : first + 9, :], by, 1)
+        return jnp.where(lane < by, here, after)
+
     for line in range(strip):
-        for chunk in range(width // LANES):
+        for chunk in range(chunks):
             cut = slice(chunk * LANES, (chunk + 1) * LANES)
-            left_rows[LEAD + chunk : LEAD + chunk + 1, :] = left_ref[line : line + 1, cut].astype(jnp.float32)
-            right_rows[LEAD + chunk : LEAD + chunk + 1, :] = right_ref[line : line + 1, cut].astype(jnp.float32)
-
-        def shifted(rows, begin):
-            first = begin // LANES
-            offset = begin - first * LANES
-            here = pltpu.roll(rows[pl.ds(first, 8), :], LANES - offset, 1)
-            after = pltpu.roll(rows[pl.ds(first + 1, 8), :], LANES - offset, 1)
-            return jnp.where(lane < LANES - offset, here, after)
-
+            at = slice(LEAD + chunk, LEAD + chunk + 1)
+            left_rows[at, :] = left_ref[line : line + 1, cut].astype(jnp.float32)
+            right_rows[at, :] = right_ref[line : line + 1, cut].astype(jnp.float32)
         for tile in range(tiles):
-            base = (LEAD + tile * per_tile) * LANES
-            left_part = shifted(left_rows, base - 3)[:LEFT_TILES]
-            right_part = shifted(right_rows, base - 3 - (MAXB * DB - 1) - ranges_ref[tile, 0])[:RIGHT_TILES]
+            first = LEAD + tile * per_tile
+            left_part = shifted(left_rows, first - 1, 3)[:LEFT_TILES]
+            right_part = shifted(right_rows, first - 3, 2 + ranges_ref[0, tile])[:RIGHT_TILES]
             piece = jnp.concatenate([left_part, right_part], 0).astype(jnp.bfloat16)
             for band in range(bands):
                 out_ref[band * tiles + tile, line] = piece
@@ -59,11 +69,18 @@
             jax.ShapeDtypeStruct((bands * tiles, strip, TILES, LANES), jnp.bfloat16),
             jax.ShapeDtypeStruct((8, LANES), jnp.int32),
         ],
-        in_specs=[VMEM, VMEM, SMEM],
+        in_specs=[HBM, HBM, HBM],
         out_specs=[VMEM, VMEM],
-        scratch_shapes=[pltpu.VMEM((rows, LANES), jnp.float32), pltpu.VMEM((rows, LANES), jnp.float32)],
+        scratch_shapes=[
+            pltpu.VMEM(left.shape, left.dtype),
+            pltpu.VMEM(right.shape, right.dtype),
+            pltpu.SMEM((2, tiles), jnp.int32),
+            pltpu.VMEM((rows, LANES), jnp.float32),
+            pltpu.VMEM((rows, LANES), jnp.float32),
+            pltpu.SemaphoreType.DMA((3,)),
+        ],
         compiler_params=pltpu.CompilerParams(vmem_limit_bytes=8 * 2**20),
-    )(left, right, ranges)
+    )(*[pltpu.with_memory_space_constraint(v, pltpu.HBM) for v in (left, right, ranges.T)])
 
 
 def ahead(values, by, axis):

time: 19.8 us -> 17.7 us (0.89)
  local copies, waits for them, and re-layouts: 2.15 us -> 0 us
    unnamed x5 -> x0, local copies, waits for them, and re-layouts: 2.15 us -> none
where the time goes in v2:
time: 17.7 us; the launch traced here: 17.5 us
  blocking collectives  14.5 us (82%)
  Pallas kernels  2.99 us (17%)
    all_to_all x1, blocking collectives, on_device(): lax.all_to_all(pieces, ('rows', 'cols'), split_axis=0, concat_axis=0, til...  14.5 us
    pallas_call x1, Pallas kernels, score(): pl.pallas_call(functools.partial(score_kernel, lines.shape[0]), out_shape...  2.15 us
    pallas_call x1, Pallas kernels, pack(): pl.pallas_call(functools.partial(pack_kernel, bands, tiles), out_shape=[j...  0.84 us

profile of v2, /device:TPU:0, one launch (start us, length us, event | category | flops | bytes accessed | tf_op | source)
XLA Modules:
  0.0 17.5 jit_solution(13994608727060904467)
XLA Ops:
  0.0 0.8 %shard_map.37 = (bf16[32,1,8,128]{3,2,1,0:T(8,128)(2,1)S(1)}, s32[8,128]{1,0:T(8,128)S(1)}) custom-call(bf16[1,2048]{1,0:T(2,128)(2,1)} %left_hbm.1, bf16[1,2048]{1,0:T(2,128)(2,1)} %right_hbm.1, s32[2,8]{1,0:T(2,128)} %bitcast.3), custom_call_target="tpu_custom_call" | custom-call | tf_op jit(solution)/shard_map/pallas_call | solution.py:66
  0.9 14.5 %all_to_all.5 = bf16[32,1,8,128]{3,2,1,0:T(8,128)(2,1)S(1)} all-to-all(bf16[32,1,8,128]{3,2,1,0:T(8,128)(2,1)S(1)} %get-tuple-element.7), channel_id=1, replica_groups=mesh['rows'=4,'cols'=8] {'rows','cols'}, dimensions={0} | all-to-all | bytes 131072 | tf_op jit(solution)/shard_map/all_to_all | solution.py:177
  15.3 2.2 %shard_map.38 = f32[8,256]{1,0:T(8,128)} custom-call(bf16[32,8,128]{2,1,0:T(8,128)(2,1)S(1)} %bitcast.2, s32[8,128]{1,0:T(8,128)S(1)} %get-tuple-element.8.low_ref), custom_call_target="tpu_custom_call" | custom-call | tf_op jit(solution)/shard_map/pallas_call | solution.py:163

commit v3 on v2

--- a/solution.py
+++ b/solution.py
@@ -84,20 +84,23 @@
 
 
 def ahead(values, by, axis):
+    if by == 0:
+        return values
     return pltpu.roll(values, values.shape[axis] - by, axis)
 
 
-def box(values, axis):
-    two = values + ahead(values, 1, axis)
-    four = two + ahead(two, 2, axis)
-    return four + ahead(two, 4, axis) + ahead(values, 6, axis)
+def column_sum(values):
+    two = values + ahead(values, 1, 0)
+    four = two + ahead(two, 2, 0)
+    return (four + ahead(two, 4, 0) + ahead(values, 6, 0))[:GROUP]
 
 
-def moments(pixels):
-    total = box(box(pixels, 1), 0)[:GROUP]
-    mean = total / 49.0
-    spread = jnp.maximum(box(box(pixels * pixels, 1), 0)[:GROUP] / 49.0 - mean * mean, 0.01)
-    return total, mean, spread
+def moments(shifted):
+    total = column_sum(sum(shifted[1:], shifted[0]))
+    squares = [v * v for v in shifted]
+    mean = total * (1.0 / 49.0)
+    spread = column_sum(sum(squares[1:], squares[0])) * (1.0 / 49.0) - mean * mean
+    return total, mean, lax.rsqrt(jnp.maximum(spread, 0.01))
 
 
 def parts(values):
@@ -105,14 +108,15 @@
     rest = values - high.astype(jnp.float32)
     middle = rest.astype(jnp.bfloat16)
     low = (rest - middle.astype(jnp.float32)).astype(jnp.bfloat16)
-    return [p.astype(jnp.float32) for p in (high, middle, low)]
+    return [high, middle, low]
 
 
 def score_kernel(height, lines_ref, low_ref, out_ref, rows):
     band_rows, tile_width = out_ref.shape
-    row = lax.broadcasted_iota(jnp.int32, (16, 1), 0)
-    row8 = lax.broadcasted_iota(jnp.int32, (GROUP, 1), 0)
+    reach = tile_width + MAXB * DB
     span = MAXB * DB + LANES
+    row = lax.broadcasted_iota(jnp.int32, (16, tile_width), 0)
+    row8 = lax.broadcasted_iota(jnp.int32, (GROUP, tile_width), 0)
     past = lax.broadcasted_iota(jnp.int32, (span, LANES), 0) - lax.broadcasted_iota(jnp.int32, (span, LANES), 1)
     inside = (past >= low_ref[0:1, :]) & (past < MAXB * DB)
     cap = jnp.where(inside, FAR, -FAR)
@@ -127,35 +131,38 @@
         tiles = [rows[pl.ds(t, 16, stride=TILES), :] for t in range(TILES)]
         left = jnp.concatenate(tiles[:LEFT_TILES], 1)
         right = jnp.concatenate(tiles[LEFT_TILES:], 1)
-        left_total, _, left_spread = moments(left)
-        _, right_mean, right_spread = moments(right)
-        reach = tile_width + MAXB * DB
-        left_scale = lax.rsqrt(left_spread[:, :tile_width]) * (1.0 / 49.0)
-        right_scale = jnp.transpose(lax.rsqrt(right_spread[:, :reach]))
-        left_parts = parts(-left_total[:, :tile_width])
-        right_parts = parts(right_mean[:, :reach])
-        shifted_left = [(left if j == 0 else ahead(left, j, 1))[:, :tile_width] for j in range(7)]
-        shifted_right = [(right if j == 0 else ahead(right, j, 1))[:, :reach] for j in range(7)]
-        right_side = jnp.concatenate(shifted_right + [b for _ in range(3) for b in right_parts], 0)
-        right_side = jnp.transpose(right_side).astype(jnp.bfloat16)
-        result = []
+        shifted_left = [ahead(left, j, 1)[:, :tile_width] for j in range(7)]
+        shifted_right = [ahead(right, j, 1)[:, :reach] for j in range(7)]
+        left_total, _, left_scale = moments(shifted_left)
+        _, right_mean, right_scale = moments(shifted_right)
+        right_scale = jnp.transpose(right_scale)
+        left_parts = [a for a in parts(-left_total) for _ in range(3)]
+        right_side = jnp.concatenate(
+            [v.astype(jnp.bfloat16) for v in shifted_right] + 3 * parts(right_mean), 0
+        )
+        right_side = jnp.transpose(right_side)
+        left_all = jnp.concatenate([v.astype(jnp.bfloat16) for v in shifted_left] + left_parts, 0)
+        scales = [jnp.broadcast_to(right_scale[:, y : y + 1], (reach, LANES)) for y in range(GROUP)]
+        sides = []
         for y in range(GROUP):
-            window = ((row >= y) & (row < y + 7)).astype(jnp.float32)
-            only = (row8 == y).astype(jnp.float32)
-            left_side = [v * window for v in shifted_left] + [a * only for a in left_parts for _ in range(3)]
-            left_side = jnp.concatenate(left_side, 0).astype(jnp.bfloat16)
-            halves = []
+            window = jnp.where((row >= y) & (row < y + 7), 1.0, 0.0).astype(jnp.bfloat16)
+            only = jnp.where(row8 == y, 1.0, 0.0).astype(jnp.bfloat16)
+            sides.append(left_all * jnp.concatenate([window] * 7 + [only] * 9, 0))
+        best = [[None] * (tile_width // LANES) for _ in range(GROUP)]
+        for y in range(0, GROUP, 2):
             for block in range(tile_width // LANES):
-                at = block * LANES
+                at = slice(block * LANES, (block + 1) * LANES)
+                reached = slice(block * LANES, block * LANES + span)
                 products = jnp.dot(
-                    right_side[at : at + span],
-                    left_side[:, at : at + LANES],
+                    right_side[reached],
+                    jnp.concatenate([sides[y][:, at], sides[y + 1][:, at]], 1),
                     preferred_element_type=jnp.float32,
                 )
-                scaled = products * right_scale[at : at + span, y : y + 1]
-                halves.append(jnp.max(jnp.minimum(scaled, cap), axis=0, keepdims=True))
-            result.append(jnp.concatenate(halves, 1))
-        best = jnp.concatenate(result, 0) * left_scale
+                for half in range(2):
+                    scaled = products[:, half * LANES : (half + 1) * LANES] * scales[y + half][reached]
+                    best[y + half][block] = jnp.max(jnp.minimum(scaled, cap), axis=0, keepdims=True)
+        best = jnp.concatenate([jnp.concatenate(b, 1) for b in best], 0)
+        best = best * (left_scale * (1.0 / 49.0))
         out_ref[group * GROUP : (group + 1) * GROUP, :] = jnp.maximum(best, -2.0)
 
 

time: 17.7 us -> 17.2 us (0.972)
  Pallas kernels: 2.99 us -> 2.53 us
    pallas_call x1, Pallas kernels: 2.15 us -> 1.69 us  [score(): pl.pallas_call(functools.partial(score_kernel, lines.shape[0]), out_shape...]
where the time goes in v3:
time: 17.2 us; the launch traced here: 17 us
  blocking collectives  14.5 us (84%)
  Pallas kernels  2.53 us (15%)
    all_to_all x1, blocking collectives, on_device(): lax.all_to_all(pieces, ('rows', 'cols'), split_axis=0, concat_axis=0, til...  14.5 us
    pallas_call x1, Pallas kernels, score(): pl.pallas_call(functools.partial(score_kernel, lines.shape[0]), out_shape...  1.69 us
    pallas_call x1, Pallas kernels, pack(): pl.pallas_call(functools.partial(pack_kernel, bands, tiles), out_shape=[j...  0.84 us

profile of v3, /device:TPU:0, one launch (start us, length us, event | category | flops | bytes accessed | tf_op | source)
XLA Modules:
  0.0 17.0 jit_solution(9131248721051056014)
XLA Ops:
  0.0 0.8 %shard_map.37 = (bf16[32,1,8,128]{3,2,1,0:T(8,128)(2,1)S(1)}, s32[8,128]{1,0:T(8,128)S(1)}) custom-call(bf16[1,2048]{1,0:T(2,128)(2,1)} %left_hbm.1, bf16[1,2048]{1,0:T(2,128)(2,1)} %right_hbm.1, s32[2,8]{1,0:T(2,128)} %bitcast.3), custom_call_target="tpu_custom_call" | custom-call | tf_op jit(solution)/shard_map/pallas_call | solution.py:66
  0.9 14.5 %all_to_all.5 = bf16[32,1,8,128]{3,2,1,0:T(8,128)(2,1)S(1)} all-to-all(bf16[32,1,8,128]{3,2,1,0:T(8,128)(2,1)S(1)} %get-tuple-element.7), channel_id=1, replica_groups=mesh['rows'=4,'cols'=8] {'rows','cols'}, dimensions={0} | all-to-all | bytes 131072 | tf_op jit(solution)/shard_map/all_to_all | solution.py:184
  15.3 1.7 %shard_map.38 = f32[8,256]{1,0:T(8,128)} custom-call(bf16[32,8,128]{2,1,0:T(8,128)(2,1)S(1)} %bitcast.2, s32[8,128]{1,0:T(8,128)S(1)} %get-tuple-element.8.low_ref), custom_call_target="tpu_custom_call" | custom-call | tf_op jit(solution)/shard_map/pallas_call | solution.py:170

commit v4 on v3

--- a/solution.py
+++ b/solution.py
@@ -15,6 +15,7 @@
 TILES = LEFT_TILES + RIGHT_TILES
 LEAD = 3
 GROUP = 8
+STEP = 32
 FAR = 3.0e37
 VMEM = pl.BlockSpec(memory_space=pltpu.VMEM)
 HBM = pl.BlockSpec(memory_space=pltpu.HBM)
@@ -96,6 +97,7 @@
 
 
 def moments(shifted):
+    shifted = [v.astype(jnp.float32) for v in shifted]
     total = column_sum(sum(shifted[1:], shifted[0]))
     squares = [v * v for v in shifted]
     mean = total * (1.0 / 49.0)
@@ -111,58 +113,114 @@
     return [high, middle, low]
 
 
+def sum_of(values):
+    return functools.reduce(lambda a, b: a + b, values)
+
+
+def fold(values):
+    return functools.reduce(jnp.maximum, [values[i : i + 8] for i in range(0, values.shape[0], 8)])
+
+
+def spread_out(values, lane_group):
+    out = []
+    for tile in range(values.shape[1] // LANES):
+        here = values[:, tile * LANES : (tile + 1) * LANES]
+        turned = [here] + [pltpu.roll(here, STEP * k, 1) for k in range(1, LANES // STEP)]
+        for g in range(LANES // STEP):
+            out.append(sum_of([turned[k] * lane_group[(g + k) % (LANES // STEP)] for k in range(LANES // STEP)]))
+    return out
+
+
+def regroup(found):
+    groups = LANES // STEP
+    row = lax.broadcasted_iota(jnp.int32, (GROUP, LANES), 0)
+    lane = lax.broadcasted_iota(jnp.int32, (GROUP, LANES), 1) // STEP
+    halves = [found[:, h * LANES : (h + 1) * LANES] for h in range(2)]
+    out = []
+    for to in range(2):
+        result = jnp.zeros((GROUP, LANES), jnp.float32)
+        for half in range(2):
+            for k in range(groups):
+                turned = halves[half] if k == 0 else pltpu.roll(halves[half], STEP * k, 1)
+                for up in sorted({(half - to) * groups - k, (half - to) * groups + (groups - k if k else 0)}):
+                    chosen = (row // groups == half) & (row - (to * groups + lane) == up)
+                    by = up % GROUP
+                    result = jnp.where(chosen, pltpu.roll(turned, by, 0) if by else turned, result)
+        out.append(result)
+    return jnp.concatenate(out, 1)
+
+
 def score_kernel(height, lines_ref, low_ref, out_ref, rows):
     band_rows, tile_width = out_ref.shape
     reach = tile_width + MAXB * DB
-    span = MAXB * DB + LANES
-    row = lax.broadcasted_iota(jnp.int32, (16, tile_width), 0)
-    row8 = lax.broadcasted_iota(jnp.int32, (GROUP, tile_width), 0)
-    past = lax.broadcasted_iota(jnp.int32, (span, LANES), 0) - lax.broadcasted_iota(jnp.int32, (span, LANES), 1)
+    span = MAXB * DB + STEP
+    taken = GROUP + 6
+    row16 = lax.broadcasted_iota(jnp.int32, (16, 2 * LANES), 0)
+    owner16 = lax.broadcasted_iota(jnp.int32, (16, 2 * LANES), 1) // STEP
+    window = jnp.where((row16 >= owner16) & (row16 < owner16 + 7), 1.0, 0.0).astype(jnp.bfloat16)
+    only = jnp.where((row16 & 7) == owner16, 1.0, 0.0)[:GROUP]
+    lane16 = lax.broadcasted_iota(jnp.int32, (16, LANES), 1) // STEP
+    lane_group = [jnp.where(lane16 == p, 1.0, 0.0) for p in range(LANES // STEP)]
+    lane_group8 = [v[:GROUP] for v in lane_group]
+    lane_group = [v.astype(jnp.bfloat16) for v in lane_group]
+    past = lax.broadcasted_iota(jnp.int32, (span, LANES), 0) - (
+        lax.broadcasted_iota(jnp.int32, (span, LANES), 1) & (STEP - 1)
+    )
     inside = (past >= low_ref[0:1, :]) & (past < MAXB * DB)
     cap = jnp.where(inside, FAR, -FAR)
+    always = (DB + STEP, MAXB * DB)
     rows[...] = jnp.zeros_like(rows)
     for group in range(band_rows // GROUP):
         first = lax.axis_index("rows") * band_rows + group * GROUP - 3
-        for i in range(GROUP + 6):
-            y = first + i
-            valid = ((y >= 0) & (y < height)).astype(jnp.float32)
-            line = lines_ref[jnp.clip(y, 0, height - 1)].astype(jnp.float32)
-            rows[i * TILES : (i + 1) * TILES, :] = line * valid
-        tiles = [rows[pl.ds(t, 16, stride=TILES), :] for t in range(TILES)]
-        left = jnp.concatenate(tiles[:LEFT_TILES], 1)
-        right = jnp.concatenate(tiles[LEFT_TILES:], 1)
+        base = jnp.clip(first, 0, height - taken)
+        if group:
+            rows[...] = jnp.zeros_like(rows)
+        found_lines = lines_ref[pl.ds(base, taken)].astype(jnp.float32)
+        rows[pl.ds(base - first + 3, taken)] = found_lines
+        flat = rows.reshape(rows.shape[0] * TILES, LANES)
+        tiles = [flat[pl.ds(3 * TILES + t, 16, stride=TILES), :] for t in range(TILES)]
+        left = jnp.concatenate(tiles[:LEFT_TILES], 1).astype(jnp.bfloat16)
+        right = jnp.concatenate(tiles[LEFT_TILES:], 1).astype(jnp.bfloat16)
+        shifted_right = [ahead(right, j, 1)[:, :reach] for j in range(7)]
         shifted_left = [ahead(left, j, 1)[:, :tile_width] for j in range(7)]
-        shifted_right = [ahead(right, j, 1)[:, :reach] for j in range(7)]
+        blank = jnp.zeros((16, reach), jnp.bfloat16)
+        near_side = jnp.transpose(jnp.concatenate(shifted_right + [blank], 0))
+        _, right_mean, right_scale = moments(shifted_right)
         left_total, _, left_scale = moments(shifted_left)
-        _, right_mean, right_scale = moments(shifted_right)
-        right_scale = jnp.transpose(right_scale)
-        left_parts = [a for a in parts(-left_total) for _ in range(3)]
-        right_side = jnp.concatenate(
-            [v.astype(jnp.bfloat16) for v in shifted_right] + 3 * parts(right_mean), 0
-        )
-        right_side = jnp.transpose(right_side)
-        left_all = jnp.concatenate([v.astype(jnp.bfloat16) for v in shifted_left] + left_parts, 0)
-        scales = [jnp.broadcast_to(right_scale[:, y : y + 1], (reach, LANES)) for y in range(GROUP)]
-        sides = []
-        for y in range(GROUP):
-            window = jnp.where((row >= y) & (row < y + 7), 1.0, 0.0).astype(jnp.bfloat16)
-            only = jnp.where(row8 == y, 1.0, 0.0).astype(jnp.bfloat16)
-            sides.append(left_all * jnp.concatenate([window] * 7 + [only] * 9, 0))
-        best = [[None] * (tile_width // LANES) for _ in range(GROUP)]
-        for y in range(0, GROUP, 2):
-            for block in range(tile_width // LANES):
-                at = slice(block * LANES, (block + 1) * LANES)
-                reached = slice(block * LANES, block * LANES + span)
-                products = jnp.dot(
-                    right_side[reached],
-                    jnp.concatenate([sides[y][:, at], sides[y + 1][:, at]], 1),
-                    preferred_element_type=jnp.float32,
-                )
-                for half in range(2):
-                    scaled = products[:, half * LANES : (half + 1) * LANES] * scales[y + half][reached]
-                    best[y + half][block] = jnp.max(jnp.minimum(scaled, cap), axis=0, keepdims=True)
-        best = jnp.concatenate([jnp.concatenate(b, 1) for b in best], 0)
-        best = best * (left_scale * (1.0 / 49.0))
+        far_side = [p.astype(jnp.float32) for p in 3 * parts(right_mean) + parts(right_scale)]
+        far_side = jnp.transpose(jnp.concatenate(far_side, 0).astype(jnp.bfloat16))
+        right_side = jnp.concatenate([near_side, far_side], 1)
+        depth = right_side.shape[1]
+        near = [spread_out(v, lane_group) for v in shifted_left]
+        far = [spread_out(p.astype(jnp.float32), lane_group8) for p in parts(-left_total)]
+        source = lax.broadcasted_iota(jnp.int32, (depth, 2 * LANES), 0)
+        owner = lax.broadcasted_iota(jnp.int32, (depth, 2 * LANES), 1) // STEP
+        picked = (source >= 128 + 9 * GROUP) & ((source & 7) == owner)
+        picks = jnp.where(picked, 1.0, 0.0).astype(jnp.bfloat16)
+        scale = jnp.dot(right_side, picks, preferred_element_type=jnp.float32)
+        none = jnp.zeros((16, 2 * LANES), jnp.bfloat16)
+        none24 = jnp.zeros((3 * GROUP, 2 * LANES), jnp.float32)
+        found = []
+        for block in range(tile_width // STEP):
+            left_side = [jnp.concatenate([v[block]] * 2, 1) * window for v in near] + [none]
+            means = [jnp.concatenate([a[block]] * 2, 1) * only for a in far for _ in range(3)]
+            left_side.append(jnp.concatenate(means + [none24], 0).astype(jnp.bfloat16))
+            reached = slice(block * STEP, block * STEP + span)
+            products = jnp.dot(
+                right_side[reached], jnp.concatenate(left_side, 0), preferred_element_type=jnp.float32
+            )
+            halves = []
+            for half in range(2):
+                at = slice(half * LANES, (half + 1) * LANES)
+                scaled = products[:, at] * scale[reached, at]
+                kept = [
+                    jnp.minimum(scaled[: always[0]], cap[: always[0]]),
+                    scaled[always[0] : always[1]],
+                    jnp.minimum(scaled[always[1] :], cap[always[1] :]),
+                ]
+                halves.append(jnp.max(functools.reduce(jnp.maximum, [fold(v) for v in kept]), axis=0, keepdims=True))
+            found.append(jnp.concatenate(halves, 1))
+        best = regroup(jnp.concatenate(found, 0)) * (left_scale * (1.0 / 49.0))
         out_ref[group * GROUP : (group + 1) * GROUP, :] = jnp.maximum(best, -2.0)
 
 
@@ -172,7 +230,7 @@
         out_shape=jax.ShapeDtypeStruct((band_rows, tile_width), jnp.float32),
         in_specs=[VMEM, VMEM],
         out_specs=VMEM,
-        scratch_shapes=[pltpu.VMEM((16 * TILES, LANES), jnp.float32)],
+        scratch_shapes=[pltpu.VMEM((GROUP + 12, TILES, LANES), jnp.float32)],
         compiler_params=pltpu.CompilerParams(vmem_limit_bytes=16 * 2**20),
     )(lines, low)
 

time: 17.2 us -> 17.1 us (level)
  no operation moved by 1% of the time
where the time goes in v4:
time: 17.1 us; the launch traced here: 16.9 us
  blocking collectives  14.5 us (85%)
  Pallas kernels  2.38 us (14%)
    all_to_all x1, blocking collectives, on_device(): lax.all_to_all(pieces, ('rows', 'cols'), split_axis=0, concat_axis=0, til...  14.5 us
    pallas_call x1, Pallas kernels, score(): pl.pallas_call(functools.partial(score_kernel, lines.shape[0]), out_shape...  1.53 us
    pallas_call x1, Pallas kernels, pack(): pl.pallas_call(functools.partial(pack_kernel, bands, tiles), out_shape=[j...  0.84 us

profile of v4, /device:TPU:0, one launch (start us, length us, event | category | flops | bytes accessed | tf_op | source)
XLA Modules:
  0.0 16.9 jit_solution(14589582951705945753)
XLA Ops:
  0.0 0.8 %shard_map.37 = (bf16[32,1,8,128]{3,2,1,0:T(8,128)(2,1)S(1)}, s32[8,128]{1,0:T(8,128)S(1)}) custom-call(bf16[1,2048]{1,0:T(2,128)(2,1)} %left_hbm.1, bf16[1,2048]{1,0:T(2,128)(2,1)} %right_hbm.1, s32[2,8]{1,0:T(2,128)} %bitcast.3), custom_call_target="tpu_custom_call" | custom-call | tf_op jit(solution)/shard_map/pallas_call | solution.py:67
  0.9 14.5 %all_to_all.5 = bf16[32,1,8,128]{3,2,1,0:T(8,128)(2,1)S(1)} all-to-all(bf16[32,1,8,128]{3,2,1,0:T(8,128)(2,1)S(1)} %get-tuple-element.7), channel_id=1, replica_groups=mesh['rows'=4,'cols'=8] {'rows','cols'}, dimensions={0} | all-to-all | bytes 131072 | tf_op jit(solution)/shard_map/all_to_all | solution.py:242
  15.3 1.5 %shard_map.38 = f32[8,256]{1,0:T(8,128)} custom-call(bf16[32,8,128]{2,1,0:T(8,128)(2,1)S(1)} %bitcast.2, s32[8,128]{1,0:T(8,128)S(1)} %get-tuple-element.8.low_ref), custom_call_target="tpu_custom_call" | custom-call | tf_op jit(solution)/shard_map/pallas_call | solution.py:228

commit v5 on v4

--- a/solution.py
+++ b/solution.py
@@ -14,6 +14,7 @@
 RIGHT_TILES = 5
 TILES = LEFT_TILES + RIGHT_TILES
 LEAD = 3
+RIGHT_LEAD = 67
 GROUP = 8
 STEP = 32
 FAR = 3.0e37
@@ -21,7 +22,35 @@
 HBM = pl.BlockSpec(memory_space=pltpu.HBM)
 
 
-def pack_kernel(bands, tiles, left_hbm, right_hbm, ranges_hbm, out_ref, low_ref, left_ref, right_ref, ranges_ref, left_rows, right_rows, sems):
+def cut(left_rows, right_rows, first):
+    lane = lax.broadcasted_iota(jnp.int32, (8, LANES), 1)
+
+    def shifted(rows, at, by):
+        here = pltpu.roll(rows[pl.ds(at, 8), :], by, 1)
+        after = pltpu.roll(rows[pl.ds(at + 1, 8), :], by, 1)
+        return jnp.where(lane < by, here, after)
+
+    left_part = shifted(left_rows, first - 1, 3)[:LEFT_TILES]
+    right_part = shifted(right_rows, first - 3, RIGHT_LEAD)[:RIGHT_TILES]
+    return jnp.concatenate([left_part, right_part], 0).astype(jnp.bfloat16)
+
+
+def cut_all(tiles, left_ref, right_ref, left_rows, right_rows, put):
+    strip, width = left_ref.shape
+    chunks = width // LANES
+    per_tile = chunks // tiles
+    core = lax.rem(lax.axis_index("cols"), 2)
+    for line in range(strip):
+        for chunk in range(chunks):
+            span = slice(chunk * LANES, (chunk + 1) * LANES)
+            at = slice(LEAD + chunk, LEAD + chunk + 1)
+            left_rows[at, :] = left_ref[line : line + 1, span].astype(jnp.float32)
+            right_rows[at, :] = right_ref[line : line + 1, span].astype(jnp.float32)
+        for pair in range(tiles // 2):
+            put(pair, line, cut(left_rows, right_rows, LEAD + (2 * pair + core) * per_tile))
+
+
+def own_kernel(tiles, left_hbm, right_hbm, ranges_hbm, out_ref, start_ref, low_ref, left_ref, right_ref, ranges_ref, left_rows, right_rows, sems):
     copies = [
         pltpu.make_async_copy(source, target, sems.at[i])
         for i, (source, target) in enumerate(
@@ -30,48 +59,32 @@
     ]
     for copy in copies:
         copy.start()
-    strip, width = left_ref.shape
-    chunks = width // LANES
-    per_tile = chunks // tiles
-    lane = lax.broadcasted_iota(jnp.int32, (8, LANES), 1)
     left_rows[...] = jnp.zeros_like(left_rows)
     right_rows[...] = jnp.zeros_like(right_rows)
     for copy in copies:
         copy.wait()
-    low = MAXB * DB - DB * ranges_ref[1, lax.axis_index("cols")]
-    low_ref[...] = jnp.full(low_ref.shape, low, jnp.int32)
-
-    def shifted(rows, first, by):
-        here = pltpu.roll(rows[first : first + 8, :], by, 1)
-        after = pltpu.roll(rows[first + 1 : first + 9, :], by, 1)
-        return jnp.where(lane < by, here, after)
-
-    for line in range(strip):
-        for chunk in range(chunks):
-            cut = slice(chunk * LANES, (chunk + 1) * LANES)
-            at = slice(LEAD + chunk, LEAD + chunk + 1)
-            left_rows[at, :] = left_ref[line : line + 1, cut].astype(jnp.float32)
-            right_rows[at, :] = right_ref[line : line + 1, cut].astype(jnp.float32)
-        for tile in range(tiles):
-            first = LEAD + tile * per_tile
-            left_part = shifted(left_rows, first - 1, 3)[:LEFT_TILES]
-            right_part = shifted(right_rows, first - 3, 2 + ranges_ref[0, tile])[:RIGHT_TILES]
-            piece = jnp.concatenate([left_part, right_part], 0).astype(jnp.bfloat16)
-            for band in range(bands):
-                out_ref[band * tiles + tile, line] = piece
-
-
-def pack(left, right, ranges, bands, tiles):
+    tile = lax.axis_index("cols")
+    start_ref[...] = jnp.full(start_ref.shape, ranges_ref[0, tile], jnp.int32)
+    low_ref[...] = jnp.full(low_ref.shape, MAXB * DB - DB * ranges_ref[1, tile], jnp.int32)
+
+    def put(pair, line, piece):
+        out_ref[pair, line] = piece
+
+    cut_all(tiles, left_ref, right_ref, left_rows, right_rows, put)
+
+
+def cut_own(left, right, ranges, tiles):
     strip, width = left.shape
     rows = LEAD + width // LANES + 13
     return pl.pallas_call(
-        functools.partial(pack_kernel, bands, tiles),
+        functools.partial(own_kernel, tiles),
         out_shape=[
-            jax.ShapeDtypeStruct((bands * tiles, strip, TILES, LANES), jnp.bfloat16),
+            jax.ShapeDtypeStruct((tiles // 2, strip, TILES, LANES), jnp.bfloat16),
+            jax.ShapeDtypeStruct((8, LANES), jnp.int32),
             jax.ShapeDtypeStruct((8, LANES), jnp.int32),
         ],
         in_specs=[HBM, HBM, HBM],
-        out_specs=[VMEM, VMEM],
+        out_specs=[VMEM, VMEM, VMEM],
         scratch_shapes=[
             pltpu.VMEM(left.shape, left.dtype),
             pltpu.VMEM(right.shape, right.dtype),
@@ -81,7 +94,37 @@
             pltpu.SemaphoreType.DMA((3,)),
         ],
         compiler_params=pltpu.CompilerParams(vmem_limit_bytes=8 * 2**20),
+        cost_estimate=pl.CostEstimate(flops=10**6, bytes_accessed=2**16, transcendentals=0),
     )(*[pltpu.with_memory_space_constraint(v, pltpu.HBM) for v in (left, right, ranges.T)])
+
+
+def pair_kernel(bands, tiles, own_ref, left_ref, right_ref, out_ref, left_rows, right_rows):
+    left_rows[...] = jnp.zeros_like(left_rows)
+    right_rows[...] = jnp.zeros_like(right_rows)
+    core = lax.rem(lax.axis_index("cols"), 2)
+    chips = bands * tiles // 2
+
+    def put(pair, line, piece):
+        mine = own_ref[pair, line]
+        for band in range(bands):
+            member = (band * (tiles // 2) + pair + 1) % chips
+            out_ref[member, core, line] = mine
+            out_ref[member, 1 - core, line] = piece
+
+    cut_all(tiles, left_ref, right_ref, left_rows, right_rows, put)
+
+
+def cut_pair(own, left, right, bands, tiles):
+    strip, width = left.shape
+    rows = LEAD + width // LANES + 13
+    return pl.pallas_call(
+        functools.partial(pair_kernel, bands, tiles),
+        out_shape=jax.ShapeDtypeStruct((bands * tiles // 2, 2, strip, TILES, LANES), jnp.bfloat16),
+        in_specs=[VMEM, VMEM, VMEM],
+        out_specs=VMEM,
+        scratch_shapes=[pltpu.VMEM((rows, LANES), jnp.float32), pltpu.VMEM((rows, LANES), jnp.float32)],
+        compiler_params=pltpu.CompilerParams(vmem_limit_bytes=8 * 2**20),
+    )(own, left, right)
 
 
 def ahead(values, by, axis):
@@ -150,7 +193,7 @@
     return jnp.concatenate(out, 1)
 
 
-def score_kernel(height, lines_ref, low_ref, out_ref, rows):
+def score_kernel(height, strip, lines_ref, start_ref, low_ref, out_ref, rows):
     band_rows, tile_width = out_ref.shape
     reach = tile_width + MAXB * DB
     span = MAXB * DB + STEP
@@ -170,18 +213,27 @@
     cap = jnp.where(inside, FAR, -FAR)
     always = (DB + STEP, MAXB * DB)
     rows[...] = jnp.zeros_like(rows)
+    start = start_ref[0, 0]
+    lane = lax.broadcasted_iota(jnp.int32, (16, LANES), 1)
+
+    def moved(pieces, by):
+        turned = [pltpu.roll(v, by, 1) for v in pieces]
+        ahead_by = [jnp.where(lane < by, a, b) for a, b in zip(turned, turned[1:])]
+        return jnp.concatenate(ahead_by, 1).astype(jnp.bfloat16)
+
     for group in range(band_rows // GROUP):
         first = lax.axis_index("rows") * band_rows + group * GROUP - 3
         base = jnp.clip(first, 0, height - taken)
         if group:
             rows[...] = jnp.zeros_like(rows)
-        found_lines = lines_ref[pl.ds(base, taken)].astype(jnp.float32)
-        rows[pl.ds(base - first + 3, taken)] = found_lines
+        into = base - first + 3
+        for count, at in ((taken - 2, 0), (2, taken - 2)):
+            part = lines_ref[pl.ds(lax.rem(base + at + 2 * strip, height), count)].astype(jnp.float32)
+            rows[pl.ds(into + at, count)] = part
         flat = rows.reshape(rows.shape[0] * TILES, LANES)
         tiles = [flat[pl.ds(3 * TILES + t, 16, stride=TILES), :] for t in range(TILES)]
         left = jnp.concatenate(tiles[:LEFT_TILES], 1).astype(jnp.bfloat16)
-        right = jnp.concatenate(tiles[LEFT_TILES:], 1).astype(jnp.bfloat16)
-        shifted_right = [ahead(right, j, 1)[:, :reach] for j in range(7)]
+        shifted_right = [moved(tiles[LEFT_TILES:], RIGHT_LEAD - 4 - j + start) for j in range(7)]
         shifted_left = [ahead(left, j, 1)[:, :tile_width] for j in range(7)]
         blank = jnp.zeros((16, reach), jnp.bfloat16)
         near_side = jnp.transpose(jnp.concatenate(shifted_right + [blank], 0))
@@ -224,24 +276,33 @@
         out_ref[group * GROUP : (group + 1) * GROUP, :] = jnp.maximum(best, -2.0)
 
 
-def score(lines, low, band_rows, tile_width):
+def score(lines, start, low, band_rows, tile_width):
     return pl.pallas_call(
-        functools.partial(score_kernel, lines.shape[0]),
+        functools.partial(score_kernel, lines.shape[0], band_rows // lax.axis_size("cols")),
         out_shape=jax.ShapeDtypeStruct((band_rows, tile_width), jnp.float32),
-        in_specs=[VMEM, VMEM],
+        in_specs=[VMEM, VMEM, VMEM],
         out_specs=VMEM,
         scratch_shapes=[pltpu.VMEM((GROUP + 12, TILES, LANES), jnp.float32)],
         compiler_params=pltpu.CompilerParams(vmem_limit_bytes=16 * 2**20),
-    )(lines, low)
+    )(lines, start, low)
 
 
 def on_device(left_image, right_image, ranges):
     bands, tiles = lax.axis_size("rows"), lax.axis_size("cols")
     strip, width = left_image.shape
-    pieces, low = pack(left_image, right_image, ranges, bands, tiles)
-    lines = lax.all_to_all(pieces, ("rows", "cols"), split_axis=0, concat_axis=0, tiled=True)
+    chips = bands * tiles // 2
+    swap = [(i, i ^ 1) for i in range(tiles)]
+    left_other = lax.ppermute(left_image, "cols", swap)
+    right_other = lax.ppermute(right_image, "cols", swap)
+    own, start, low = cut_own(left_image, right_image, ranges, tiles)
+    pieces = cut_pair(own, left_other, right_other, bands, tiles)
+    order = [chips - 1] + list(range(chips - 1))
+    groups = [[2 * chip + core for chip in order] for core in range(2)]
+    lines = lax.all_to_all(
+        pieces, ("rows", "cols"), split_axis=0, concat_axis=0, tiled=True, axis_index_groups=groups
+    )
     lines = lines.reshape(bands * tiles * strip, TILES, LANES)
-    return score(lines, low, strip * tiles, width // tiles)
+    return score(lines, start, low, strip * tiles, width // tiles)
 
 
 def solution(mesh):

time: 17.1 us -> 15.7 us (0.918)
  blocking collectives: 14.5 us -> 12 us
  starting transfers between devices: 0 us -> 0.51 us
  waiting for transfers between devices: 0 us -> 0.48 us
    all_to_all x1, blocking collectives: 14.5 us -> 12 us  [on_device(): lax.all_to_all(pieces, ('rows', 'cols'), split_axis=0, concat_axis=0, til...]
    ppermute x0 -> x2, starting transfers between devices: none -> 0.51 us  [the longest x1 0.45 us: on_device(): left_other = lax.ppermute(left_image, 'cols', swap)]
    ppermute x0 -> x2, waiting for transfers between devices: none -> 0.48 us  [the longest x1 0.34 us: on_device(): right_other = lax.ppermute(right_image, 'cols', swap)]
    pallas_call x2 -> x3, Pallas kernels: 2.38 us -> 2.49 us  [the longest x1 1.56 us: score(): pl.pallas_call(functools.partial(score_kernel, lines.shape[0], band_rows...]
  transfers between devices with their start and end apart: 0 -> 2, of which waited for: 0 -> 2; matrix products, arithmetic and copies ran while one was open for 0% -> 0% of each run, Pallas kernels for 0% -> 5%
where the time goes in v5:
time: 15.7 us; the launch traced here: 15.5 us
  blocking collectives  12 us (76%)
  Pallas kernels  2.49 us (16%)
  starting transfers between devices  0.51 us (3%)
  waiting for transfers between devices  0.48 us (3%)
    all_to_all x1, blocking collectives, on_device(): lax.all_to_all(pieces, ('rows', 'cols'), split_axis=0, concat_axis=0, til...  12 us
    pallas_call x1, Pallas kernels, score(): pl.pallas_call(functools.partial(score_kernel, lines.shape[0], band_rows...  1.56 us
    pallas_call x1, Pallas kernels, cut_own(): pl.pallas_call(functools.partial(own_kernel, tiles), out_shape=[jax.Shape...  0.83 us
    ppermute x1, starting transfers between devices, on_device(): left_other = lax.ppermute(left_image, 'cols', swap)  0.45 us
    ppermute x1, waiting for transfers between devices, on_device(): right_other = lax.ppermute(right_image, 'cols', swap)  0.34 us
  transfers between devices with their start and end apart: 2, of which 2 were waited for; matrix products, arithmetic and copies ran while one was open for 0% of the time, Pallas kernels for 5%

profile of v5, /device:TPU:0, one launch (start us, length us, event | category | flops | bytes accessed | tf_op | source)
XLA Modules:
  0.0 15.5 jit_solution(1386812636484656312)
XLA Ops:
  0.0 0.5 %collective-permute-start = (bf16[1,2048]{1,0:T(2,128)(2,1)}, bf16[1,2048]{1,0:T(2,128)(2,1)S(1)}, u32[]{:S(2)}, u32[]{:S(2)}) collective-permute-start(bf16[1,2048]{1,0:T(2,128)(2,1)} %left_hbm.1), channel_id=1, source_target_pairs={{0,1},{1,0},{2,3},{3,2},{4,5},{5,4},{6,7},{7,6},{8,9},{9,8},{10,11... | collective-permute-start | bytes 12296 | tf_op jit(solution)/shard_map/ppermute | solution.py:295
  0.5 0.1 collective-permute-start.1
  0.5 0.8 %shard_map.37 = (bf16[4,1,8,128]{3,2,1,0:T(8,128)(2,1)S(1)}, s32[8,128]{1,0:T(8,128)S(1)}, s32[8,128]{1,0:T(8,128)S(1)}) custom-call(bf16[1,2048]{1,0:T(2,128)(2,1)} %left_hbm.1, bf16[1,2048]{1,0:T(2,128)(2,1)} %right_hbm.1, s32[2,8]{1,0:T(2,128)} %bitcast.3), custom_call_target="tpu_custom_call" | custom-call | flops 1000000 | bytes 65536 | tf_op jit(solution)/shard_map/pallas_call | solution.py:79
  1.4 0.1 collective-permute-done.left_ref
  1.5 0.3 %collective-permute-done.1.right_ref = bf16[1,2048]{1,0:T(2,128)(2,1)S(1)} collective-permute-done((bf16[1,2048]{1,0:T(2,128)(2,1)}, bf16[1,2048]{1,0:T(2,128)(2,1)S(1)}, u32[]{:S(2)}, u32[]{:S(2)}) %collective-permute-start.1) | collective-permute-done | bytes 4128 | tf_op jit(solution)/shard_map/ppermute | solution.py:296
  1.8 0.1 shard_map.38
  1.9 12.0 %all_to_all.5 = bf16[16,2,1,8,128]{4,3,2,1,0:T(8,128)(2,1)S(1)} all-to-all(bf16[16,2,1,8,128]{4,3,2,1,0:T(8,128)(2,1)S(1)} %shard_map.38), channel_id=1, replica_groups={{30,0,2,4,6,8,10,12,14,16,18,20,22,24,26,28},{31,1,3,5,7,9,11,13,15,17,..., dimensions={0} | all-to-all | bytes 131072 | tf_op jit(solution)/shard_map/all_to_all | solution.py:301
  14.0 1.6 %shard_map.39 = f32[8,256]{1,0:T(8,128)} custom-call(bf16[32,8,128]{2,1,0:T(8,128)(2,1)S(1)} %bitcast.2, s32[8,128]{1,0:T(8,128)S(1)} %get-tuple-element.9.start_ref, s32[8,128]{1,0:T(8,128)S(1)} %get-tuple-element.10.low_ref), custom_call_target="tpu_custom_call" | custom-call | tf_op jit(solution)/shard_map/pallas_call | solution.py:280
Async XLA Ops:
  0.0 1.5 %collective-permute-start = (bf16[1,2048]{1,0:T(2,128)(2,1)}, bf16[1,2048]{1,0:T(2,128)(2,1)S(1)}, u32[]{:S(2)}, u32[]{:S(2)}) collective-permute-start(bf16[1,2048]{1,0:T(2,128)(2,1)} %left_hbm.1), channel_id=1, source_target_pairs={{0,1},{1,0},{2,3},{3,2},{4,5},{5,4},{6,7},{7,6},{8,9},{9,8},{10,11... | collective-permute-start | bytes 12296 | tf_op jit(solution)/shard_map/ppermute | solution.py:295
  0.5 1.4 %collective-permute-start.1 = (bf16[1,2048]{1,0:T(2,128)(2,1)}, bf16[1,2048]{1,0:T(2,128)(2,1)S(1)}, u32[]{:S(2)}, u32[]{:S(2)}) collective-permute-start(bf16[1,2048]{1,0:T(2,128)(2,1)} %right_hbm.1), channel_id=1, source_target_pairs={{0,1},{1,0},{2,3},{3,2},{4,5},{5,4},{6,7},{7,6},{8,9},{9,8},{10,11... | collective-permute-start | bytes 12296 | tf_op jit(solution)/shard_map/ppermute | solution.py:296

commit v6 on v5

--- a/solution.py
+++ b/solution.py
@@ -15,6 +15,7 @@
 TILES = LEFT_TILES + RIGHT_TILES
 LEAD = 3
 RIGHT_LEAD = 67
+AHEAD = 2
 GROUP = 8
 STEP = 32
 FAR = 3.0e37
@@ -22,6 +23,10 @@
 HBM = pl.BlockSpec(memory_space=pltpu.HBM)
 
 
+def side_of(tile):
+    return lax.rem(tile + jnp.where(tile < 2, 1, 0), 2)
+
+
 def cut(left_rows, right_rows, first):
     lane = lax.broadcasted_iota(jnp.int32, (8, LANES), 1)
 
@@ -39,7 +44,7 @@
     strip, width = left_ref.shape
     chunks = width // LANES
     per_tile = chunks // tiles
-    core = lax.rem(lax.axis_index("cols"), 2)
+    side = side_of(lax.axis_index("cols"))
     for line in range(strip):
         for chunk in range(chunks):
             span = slice(chunk * LANES, (chunk + 1) * LANES)
@@ -47,7 +52,8 @@
             left_rows[at, :] = left_ref[line : line + 1, span].astype(jnp.float32)
             right_rows[at, :] = right_ref[line : line + 1, span].astype(jnp.float32)
         for pair in range(tiles // 2):
-            put(pair, line, cut(left_rows, right_rows, LEAD + (2 * pair + core) * per_tile))
+            tile = 2 * pair + (side if pair else 1 - side)
+            put(pair, line, cut(left_rows, right_rows, LEAD + tile * per_tile))
 
 
 def own_kernel(tiles, left_hbm, right_hbm, ranges_hbm, out_ref, start_ref, low_ref, left_ref, right_ref, ranges_ref, left_rows, right_rows, sems):
@@ -107,7 +113,7 @@
     def put(pair, line, piece):
         mine = own_ref[pair, line]
         for band in range(bands):
-            member = (band * (tiles // 2) + pair + 1) % chips
+            member = (band * (tiles // 2) + pair + AHEAD) % chips
             out_ref[member, core, line] = mine
             out_ref[member, 1 - core, line] = piece
 
@@ -227,8 +233,9 @@
         if group:
             rows[...] = jnp.zeros_like(rows)
         into = base - first + 3
-        for count, at in ((taken - 2, 0), (2, taken - 2)):
-            part = lines_ref[pl.ds(lax.rem(base + at + 2 * strip, height), count)].astype(jnp.float32)
+        last = 2 * AHEAD * strip
+        for count, at in ((taken - last, 0), (last, taken - last)):
+            part = lines_ref[pl.ds(lax.rem(base + at + last, height), count)].astype(jnp.float32)
             rows[pl.ds(into + at, count)] = part
         flat = rows.reshape(rows.shape[0] * TILES, LANES)
         tiles = [flat[pl.ds(3 * TILES + t, 16, stride=TILES), :] for t in range(TILES)]
@@ -296,8 +303,8 @@
     right_other = lax.ppermute(right_image, "cols", swap)
     own, start, low = cut_own(left_image, right_image, ranges, tiles)
     pieces = cut_pair(own, left_other, right_other, bands, tiles)
-    order = [chips - 1] + list(range(chips - 1))
-    groups = [[2 * chip + core for chip in order] for core in range(2)]
+    order = [(place - AHEAD) % chips for place in range(chips)]
+    groups = [[2 * chip + (side if chip % (tiles // 2) else 1 - side) for chip in order] for side in range(2)]
     lines = lax.all_to_all(
         pieces, ("rows", "cols"), split_axis=0, concat_axis=0, tiled=True, axis_index_groups=groups
     )

time: 15.7 us -> 15 us (0.955)
  the two profiles are of different devices: /device:TPU:0 before, /device:TPU:1 now
where the time goes in v6:
time: 15 us; the launch traced here: 14.8 us
  blocking collectives  11.6 us (77%)
  Pallas kernels  2.5 us (17%)
  starting transfers between devices  0.51 us (3%)
  waiting for transfers between devices  0.19 us (1%)
    all_to_all x1, blocking collectives, on_device(): lax.all_to_all(pieces, ('rows', 'cols'), split_axis=0, concat_axis=0, til...  11.6 us
    pallas_call x1, Pallas kernels, score(): pl.pallas_call(functools.partial(score_kernel, lines.shape[0], band_rows...  1.56 us
    pallas_call x1, Pallas kernels, cut_own(): pl.pallas_call(functools.partial(own_kernel, tiles), out_shape=[jax.Shape...  0.84 us
    ppermute x1, starting transfers between devices, on_device(): right_other = lax.ppermute(right_image, 'cols', swap)  0.45 us
  transfers between devices with their start and end apart: 2, of which 1 were waited for; matrix products, arithmetic and copies ran while one was open for 0% of the time, Pallas kernels for 6%

profile of v6, /device:TPU:1, one launch (start us, length us, event | category | flops | bytes accessed | tf_op | source)
XLA Modules:
  0.0 14.8 jit_solution(12195553711172816855)
XLA Ops:
  0.0 0.1 collective-permute-start
  0.1 0.5 %collective-permute-start.1 = (bf16[1,2048]{1,0:T(2,128)(2,1)}, bf16[1,2048]{1,0:T(2,128)(2,1)S(1)}, u32[]{:S(2)}, u32[]{:S(2)}) collective-permute-start(bf16[1,2048]{1,0:T(2,128)(2,1)} %right_hbm.1), channel_id=1, source_target_pairs={{0,1},{1,0},{2,3},{3,2},{4,5},{5,4},{6,7},{7,6},{8,9},{9,8},{10,11... | collective-permute-start | bytes 12296 | tf_op jit(solution)/shard_map/ppermute | solution.py:303
  0.5 0.8 %shard_map.37 = (bf16[4,1,8,128]{3,2,1,0:T(8,128)(2,1)S(1)}, s32[8,128]{1,0:T(8,128)S(1)}, s32[8,128]{1,0:T(8,128)S(1)}) custom-call(bf16[1,2048]{1,0:T(2,128)(2,1)} %left_hbm.1, bf16[1,2048]{1,0:T(2,128)(2,1)} %right_hbm.1, s32[2,8]{1,0:T(2,128)} %bitcast.3), custom_call_target="tpu_custom_call" | custom-call | flops 1000000 | bytes 65536 | tf_op jit(solution)/shard_map/pallas_call | solution.py:85
  1.4 0.0 collective-permute-done.left_ref
  1.4 0.2 %collective-permute-done.1.right_ref = bf16[1,2048]{1,0:T(2,128)(2,1)S(1)} collective-permute-done((bf16[1,2048]{1,0:T(2,128)(2,1)}, bf16[1,2048]{1,0:T(2,128)(2,1)S(1)}, u32[]{:S(2)}, u32[]{:S(2)}) %collective-permute-start.1) | collective-permute-done | bytes 4128 | tf_op jit(solution)/shard_map/ppermute | solution.py:303
  1.6 0.1 shard_map.38
  1.7 11.6 %all_to_all.5 = bf16[16,2,1,8,128]{4,3,2,1,0:T(8,128)(2,1)S(1)} all-to-all(bf16[16,2,1,8,128]{4,3,2,1,0:T(8,128)(2,1)S(1)} %shard_map.38), channel_id=1, replica_groups={{28,30,1,2,4,6,9,10,12,14,17,18,20,22,25,26},{29,31,0,3,5,7,8,11,13,15,..., dimensions={0} | all-to-all | bytes 131072 | tf_op jit(solution)/shard_map/all_to_all | solution.py:308
  13.2 1.6 %shard_map.39 = f32[8,256]{1,0:T(8,128)} custom-call(bf16[32,8,128]{2,1,0:T(8,128)(2,1)S(1)} %bitcast.2, s32[8,128]{1,0:T(8,128)S(1)} %get-tuple-element.9.start_ref, s32[8,128]{1,0:T(8,128)S(1)} %get-tuple-element.10.low_ref), custom_call_target="tpu_custom_call" | custom-call | tf_op jit(solution)/shard_map/pallas_call | solution.py:287
Async XLA Ops:
  0.0 1.4 %collective-permute-start = (bf16[1,2048]{1,0:T(2,128)(2,1)}, bf16[1,2048]{1,0:T(2,128)(2,1)S(1)}, u32[]{:S(2)}, u32[]{:S(2)}) collective-permute-start(bf16[1,2048]{1,0:T(2,128)(2,1)} %left_hbm.1), channel_id=1, source_target_pairs={{0,1},{1,0},{2,3},{3,2},{4,5},{5,4},{6,7},{7,6},{8,9},{9,8},{10,11... | collective-permute-start | bytes 12296 | tf_op jit(solution)/shard_map/ppermute | solution.py:302
  0.1 1.5 %collective-permute-start.1 = (bf16[1,2048]{1,0:T(2,128)(2,1)}, bf16[1,2048]{1,0:T(2,128)(2,1)S(1)}, u32[]{:S(2)}, u32[]{:S(2)}) collective-permute-start(bf16[1,2048]{1,0:T(2,128)(2,1)} %right_hbm.1), channel_id=1, source_target_pairs={{0,1},{1,0},{2,3},{3,2},{4,5},{5,4},{6,7},{7,6},{8,9},{9,8},{10,11... | collective-permute-start | bytes 12296 | tf_op jit(solution)/shard_map/ppermute | solution.py:303

commit v7 on v6

--- a/solution.py
+++ b/solution.py
@@ -15,12 +15,24 @@
 TILES = LEFT_TILES + RIGHT_TILES
 LEAD = 3
 RIGHT_LEAD = 67
-AHEAD = 2
 GROUP = 8
 STEP = 32
 FAR = 3.0e37
 VMEM = pl.BlockSpec(memory_space=pltpu.VMEM)
 HBM = pl.BlockSpec(memory_space=pltpu.HBM)
+
+
+def chip_order(bands, pairs):
+    chips = bands * pairs
+    leader = chips - 2
+    away = {chip: bin(chip // pairs).count("1") + chip % pairs for chip in range(1, chips)}
+    far_first = sorted(away, key=lambda chip: (-away[chip], chip != leader, chip))
+    steps = list(range(2, chips, 2)) + list(range(1, chips, 2))
+    first = -steps[far_first.index(leader)] % chips
+    order = [0] * chips
+    for step, chip in zip(steps, far_first):
+        order[(first + step) % chips] = chip
+    return order
 
 
 def side_of(tile):
@@ -108,12 +120,12 @@
     left_rows[...] = jnp.zeros_like(left_rows)
     right_rows[...] = jnp.zeros_like(right_rows)
     core = lax.rem(lax.axis_index("cols"), 2)
-    chips = bands * tiles // 2
+    order = chip_order(bands, tiles // 2)
 
     def put(pair, line, piece):
         mine = own_ref[pair, line]
         for band in range(bands):
-            member = (band * (tiles // 2) + pair + AHEAD) % chips
+            member = order.index(band * (tiles // 2) + pair)
             out_ref[member, core, line] = mine
             out_ref[member, 1 - core, line] = piece
 
@@ -199,11 +211,10 @@
     return jnp.concatenate(out, 1)
 
 
-def score_kernel(height, strip, lines_ref, start_ref, low_ref, out_ref, rows):
+def score_kernel(order, lines_ref, start_ref, low_ref, out_ref, rows):
     band_rows, tile_width = out_ref.shape
     reach = tile_width + MAXB * DB
     span = MAXB * DB + STEP
-    taken = GROUP + 6
     row16 = lax.broadcasted_iota(jnp.int32, (16, 2 * LANES), 0)
     owner16 = lax.broadcasted_iota(jnp.int32, (16, 2 * LANES), 1) // STEP
     window = jnp.where((row16 >= owner16) & (row16 < owner16 + 7), 1.0, 0.0).astype(jnp.bfloat16)
@@ -218,7 +229,14 @@
     inside = (past >= low_ref[0:1, :]) & (past < MAXB * DB)
     cap = jnp.where(inside, FAR, -FAR)
     always = (DB + STEP, MAXB * DB)
-    rows[...] = jnp.zeros_like(rows)
+    height = lines_ref.shape[0]
+    each = height // len(order)
+    rows[:3] = jnp.zeros((3, TILES, LANES), jnp.float32)
+    rows[height + 3 :] = jnp.zeros((5, TILES, LANES), jnp.float32)
+    for member, chip in enumerate(order):
+        for line in range(each):
+            rows[3 + chip * each + line] = lines_ref[member * each + line].astype(jnp.float32)
+    flat = rows.reshape(rows.shape[0] * TILES, LANES)
     start = start_ref[0, 0]
     lane = lax.broadcasted_iota(jnp.int32, (16, LANES), 1)
 
@@ -228,17 +246,8 @@
         return jnp.concatenate(ahead_by, 1).astype(jnp.bfloat16)
 
     for group in range(band_rows // GROUP):
-        first = lax.axis_index("rows") * band_rows + group * GROUP - 3
-        base = jnp.clip(first, 0, height - taken)
-        if group:
-            rows[...] = jnp.zeros_like(rows)
-        into = base - first + 3
-        last = 2 * AHEAD * strip
-        for count, at in ((taken - last, 0), (last, taken - last)):
-            part = lines_ref[pl.ds(lax.rem(base + at + last, height), count)].astype(jnp.float32)
-            rows[pl.ds(into + at, count)] = part
-        flat = rows.reshape(rows.shape[0] * TILES, LANES)
-        tiles = [flat[pl.ds(3 * TILES + t, 16, stride=TILES), :] for t in range(TILES)]
+        first = (lax.axis_index("rows") * band_rows + group * GROUP) * TILES
+        tiles = [flat[pl.ds(first + t, 16, stride=TILES), :] for t in range(TILES)]
         left = jnp.concatenate(tiles[:LEFT_TILES], 1).astype(jnp.bfloat16)
         shifted_right = [moved(tiles[LEFT_TILES:], RIGHT_LEAD - 4 - j + start) for j in range(7)]
         shifted_left = [ahead(left, j, 1)[:, :tile_width] for j in range(7)]
@@ -283,13 +292,13 @@
         out_ref[group * GROUP : (group + 1) * GROUP, :] = jnp.maximum(best, -2.0)
 
 
-def score(lines, start, low, band_rows, tile_width):
+def score(lines, start, low, order, band_rows, tile_width):
     return pl.pallas_call(
-        functools.partial(score_kernel, lines.shape[0], band_rows // lax.axis_size("cols")),
+        functools.partial(score_kernel, order),
         out_shape=jax.ShapeDtypeStruct((band_rows, tile_width), jnp.float32),
         in_specs=[VMEM, VMEM, VMEM],
         out_specs=VMEM,
-        scratch_shapes=[pltpu.VMEM((GROUP + 12, TILES, LANES), jnp.float32)],
+        scratch_shapes=[pltpu.VMEM((lines.shape[0] + 8, TILES, LANES), jnp.float32)],
         compiler_params=pltpu.CompilerParams(vmem_limit_bytes=16 * 2**20),
     )(lines, start, low)
 
@@ -297,19 +306,18 @@
 def on_device(left_image, right_image, ranges):
     bands, tiles = lax.axis_size("rows"), lax.axis_size("cols")
     strip, width = left_image.shape
-    chips = bands * tiles // 2
     swap = [(i, i ^ 1) for i in range(tiles)]
     left_other = lax.ppermute(left_image, "cols", swap)
     right_other = lax.ppermute(right_image, "cols", swap)
     own, start, low = cut_own(left_image, right_image, ranges, tiles)
     pieces = cut_pair(own, left_other, right_other, bands, tiles)
-    order = [(place - AHEAD) % chips for place in range(chips)]
+    order = chip_order(bands, tiles // 2)
     groups = [[2 * chip + (side if chip % (tiles // 2) else 1 - side) for chip in order] for side in range(2)]
     lines = lax.all_to_all(
         pieces, ("rows", "cols"), split_axis=0, concat_axis=0, tiled=True, axis_index_groups=groups
     )
     lines = lines.reshape(bands * tiles * strip, TILES, LANES)
-    return score(lines, start, low, strip * tiles, width // tiles)
+    return score(lines, start, low, order, strip * tiles, width // tiles)
 
 
 def solution(mesh):

time: 15 us -> 14.8 us (0.987)
  blocking collectives: 11.6 us -> 11.3 us
    all_to_all x1, blocking collectives: 11.6 us -> 11.3 us  [on_device(): lax.all_to_all(pieces, ('rows', 'cols'), split_axis=0, concat_axis=0, til...]
where the time goes in v7:
time: 14.8 us; the launch traced here: 14.5 us
  blocking collectives  11.3 us (76%)
  Pallas kernels  2.5 us (17%)
  starting transfers between devices  0.51 us (3%)
  waiting for transfers between devices  0.19 us (1%)
    all_to_all x1, blocking collectives, on_device(): lax.all_to_all(pieces, ('rows', 'cols'), split_axis=0, concat_axis=0, til...  11.3 us
    pallas_call x1, Pallas kernels, score(): pl.pallas_call(functools.partial(score_kernel, order), out_shape=jax.Shap...  1.56 us
    pallas_call x1, Pallas kernels, cut_own(): pl.pallas_call(functools.partial(own_kernel, tiles), out_shape=[jax.Shape...  0.84 us
    ppermute x1, starting transfers between devices, on_device(): right_other = lax.ppermute(right_image, 'cols', swap)  0.45 us
  transfers between devices with their start and end apart: 2, of which 1 were waited for; matrix products, arithmetic and copies ran while one was open for 0% of the time, Pallas kernels for 6%

profile of v7, /device:TPU:1, one launch (start us, length us, event | category | flops | bytes accessed | tf_op | source)
XLA Modules:
  0.0 14.5 jit_solution(13028843510367826889)
XLA Ops:
  0.0 0.1 collective-permute-start
  0.1 0.5 %collective-permute-start.1 = (bf16[1,2048]{1,0:T(2,128)(2,1)}, bf16[1,2048]{1,0:T(2,128)(2,1)S(1)}, u32[]{:S(2)}, u32[]{:S(2)}) collective-permute-start(bf16[1,2048]{1,0:T(2,128)(2,1)} %right_hbm.1), channel_id=1, source_target_pairs={{0,1},{1,0},{2,3},{3,2},{4,5},{5,4},{6,7},{7,6},{8,9},{9,8},{10,11... | collective-permute-start | bytes 12296 | tf_op jit(solution)/shard_map/ppermute | solution.py:311
  0.5 0.8 %shard_map.37 = (bf16[4,1,8,128]{3,2,1,0:T(8,128)(2,1)S(1)}, s32[8,128]{1,0:T(8,128)S(1)}, s32[8,128]{1,0:T(8,128)S(1)}) custom-call(bf16[1,2048]{1,0:T(2,128)(2,1)} %left_hbm.1, bf16[1,2048]{1,0:T(2,128)(2,1)} %right_hbm.1, s32[2,8]{1,0:T(2,128)} %bitcast.3), custom_call_target="tpu_custom_call" | custom-call | flops 1000000 | bytes 65536 | tf_op jit(solution)/shard_map/pallas_call | solution.py:97
  1.4 0.0 collective-permute-done.left_ref
  1.4 0.2 %collective-permute-done.1.right_ref = bf16[1,2048]{1,0:T(2,128)(2,1)S(1)} collective-permute-done((bf16[1,2048]{1,0:T(2,128)(2,1)}, bf16[1,2048]{1,0:T(2,128)(2,1)S(1)}, u32[]{:S(2)}, u32[]{:S(2)}) %collective-permute-start.1) | collective-permute-done | bytes 4128 | tf_op jit(solution)/shard_map/ppermute | solution.py:311
  1.6 0.1 shard_map.38
  1.7 11.3 %all_to_all.5 = bf16[16,2,1,8,128]{4,3,2,1,0:T(8,128)(2,1)S(1)} all-to-all(bf16[16,2,1,8,128]{4,3,2,1,0:T(8,128)(2,1)S(1)} %shard_map.38), channel_id=1, replica_groups={{28,10,14,18,22,25,6,2,12,9,20,17,1,26,30,4},{29,11,15,19,23,24,7,3,13,..., dimensions={0} | all-to-all | bytes 131072 | tf_op jit(solution)/shard_map/all_to_all | solution.py:316
  13.0 1.6 %shard_map.39 = f32[8,256]{1,0:T(8,128)} custom-call(bf16[32,8,128]{2,1,0:T(8,128)(2,1)S(1)} %bitcast.2, s32[8,128]{1,0:T(8,128)S(1)} %get-tuple-element.9.start_ref, s32[8,128]{1,0:T(8,128)S(1)} %get-tuple-element.10.low_ref), custom_call_target="tpu_custom_call" | custom-call | tf_op jit(solution)/shard_map/pallas_call | solution.py:296
Async XLA Ops:
  0.0 1.4 %collective-permute-start = (bf16[1,2048]{1,0:T(2,128)(2,1)}, bf16[1,2048]{1,0:T(2,128)(2,1)S(1)}, u32[]{:S(2)}, u32[]{:S(2)}) collective-permute-start(bf16[1,2048]{1,0:T(2,128)(2,1)} %left_hbm.1), channel_id=1, source_target_pairs={{0,1},{1,0},{2,3},{3,2},{4,5},{5,4},{6,7},{7,6},{8,9},{9,8},{10,11... | collective-permute-start | bytes 12296 | tf_op jit(solution)/shard_map/ppermute | solution.py:310
  0.1 1.5 %collective-permute-start.1 = (bf16[1,2048]{1,0:T(2,128)(2,1)}, bf16[1,2048]{1,0:T(2,128)(2,1)S(1)}, u32[]{:S(2)}, u32[]{:S(2)}) collective-permute-start(bf16[1,2048]{1,0:T(2,128)(2,1)} %right_hbm.1), channel_id=1, source_target_pairs={{0,1},{1,0},{2,3},{3,2},{4,5},{5,4},{6,7},{7,6},{8,9},{9,8},{10,11... | collective-permute-start | bytes 12296 | tf_op jit(solution)/shard_map/ppermute | solution.py:311

commit v8 on v7

--- a/solution.py
+++ b/solution.py
@@ -188,7 +188,10 @@
         here = values[:, tile * LANES : (tile + 1) * LANES]
         turned = [here] + [pltpu.roll(here, STEP * k, 1) for k in range(1, LANES // STEP)]
         for g in range(LANES // STEP):
-            out.append(sum_of([turned[k] * lane_group[(g + k) % (LANES // STEP)] for k in range(LANES // STEP)]))
+            block = turned[0]
+            for k in range(1, LANES // STEP):
+                block = jnp.where(lane_group[(g + k) % (LANES // STEP)] > 0, turned[k], block)
+            out.append(block)
     return out
 
 
@@ -218,10 +221,9 @@
     row16 = lax.broadcasted_iota(jnp.int32, (16, 2 * LANES), 0)
     owner16 = lax.broadcasted_iota(jnp.int32, (16, 2 * LANES), 1) // STEP
     window = jnp.where((row16 >= owner16) & (row16 < owner16 + 7), 1.0, 0.0).astype(jnp.bfloat16)
-    only = jnp.where((row16 & 7) == owner16, 1.0, 0.0)[:GROUP]
+    only = jnp.where((row16 & 7) == owner16, 1.0, 0.0).astype(jnp.bfloat16)
     lane16 = lax.broadcasted_iota(jnp.int32, (16, LANES), 1) // STEP
     lane_group = [jnp.where(lane16 == p, 1.0, 0.0) for p in range(LANES // STEP)]
-    lane_group8 = [v[:GROUP] for v in lane_group]
     lane_group = [v.astype(jnp.bfloat16) for v in lane_group]
     past = lax.broadcasted_iota(jnp.int32, (span, LANES), 0) - (
         lax.broadcasted_iota(jnp.int32, (span, LANES), 1) & (STEP - 1)
@@ -231,12 +233,12 @@
     always = (DB + STEP, MAXB * DB)
     height = lines_ref.shape[0]
     each = height // len(order)
-    rows[:3] = jnp.zeros((3, TILES, LANES), jnp.float32)
-    rows[height + 3 :] = jnp.zeros((5, TILES, LANES), jnp.float32)
+    rows[: 3 * TILES] = jnp.zeros((3 * TILES, LANES), jnp.float32)
+    rows[(height + 3) * TILES :] = jnp.zeros((6 * TILES, LANES), jnp.float32)
     for member, chip in enumerate(order):
         for line in range(each):
-            rows[3 + chip * each + line] = lines_ref[member * each + line].astype(jnp.float32)
-    flat = rows.reshape(rows.shape[0] * TILES, LANES)
+            at = (3 + chip * each + line) * TILES
+            rows[at : at + TILES] = lines_ref[member * each + line].astype(jnp.float32)
     start = start_ref[0, 0]
     lane = lax.broadcasted_iota(jnp.int32, (16, LANES), 1)
 
@@ -247,7 +249,7 @@
 
     for group in range(band_rows // GROUP):
         first = (lax.axis_index("rows") * band_rows + group * GROUP) * TILES
-        tiles = [flat[pl.ds(first + t, 16, stride=TILES), :] for t in range(TILES)]
+        tiles = [rows[pl.ds(first + t, 16, stride=TILES), :] for t in range(TILES)]
         left = jnp.concatenate(tiles[:LEFT_TILES], 1).astype(jnp.bfloat16)
         shifted_right = [moved(tiles[LEFT_TILES:], RIGHT_LEAD - 4 - j + start) for j in range(7)]
         shifted_left = [ahead(left, j, 1)[:, :tile_width] for j in range(7)]
@@ -255,24 +257,28 @@
         near_side = jnp.transpose(jnp.concatenate(shifted_right + [blank], 0))
         _, right_mean, right_scale = moments(shifted_right)
         left_total, _, left_scale = moments(shifted_left)
-        far_side = [p.astype(jnp.float32) for p in 3 * parts(right_mean) + parts(right_scale)]
+        high, middle, low = [p.astype(jnp.float32) for p in parts(right_mean)]
+        far_side = [high, high, middle, middle, low, low, high, middle, low, jnp.zeros_like(low)]
+        far_side += [p.astype(jnp.float32) for p in parts(right_scale)] + [jnp.zeros_like(low)]
         far_side = jnp.transpose(jnp.concatenate(far_side, 0).astype(jnp.bfloat16))
         right_side = jnp.concatenate([near_side, far_side], 1)
         depth = right_side.shape[1]
         near = [spread_out(v, lane_group) for v in shifted_left]
-        far = [spread_out(p.astype(jnp.float32), lane_group8) for p in parts(-left_total)]
+        high, middle, low = [p.astype(jnp.float32) for p in parts(-left_total)]
+        far = [jnp.concatenate(p, 0).astype(jnp.bfloat16) for p in ((high, middle), (low, low))]
+        far = [spread_out(p, lane_group) for p in far]
         source = lax.broadcasted_iota(jnp.int32, (depth, 2 * LANES), 0)
         owner = lax.broadcasted_iota(jnp.int32, (depth, 2 * LANES), 1) // STEP
-        picked = (source >= 128 + 9 * GROUP) & ((source & 7) == owner)
+        picked = (source >= 128 + 10 * GROUP) & ((source & 7) == owner)
         picks = jnp.where(picked, 1.0, 0.0).astype(jnp.bfloat16)
         scale = jnp.dot(right_side, picks, preferred_element_type=jnp.float32)
         none = jnp.zeros((16, 2 * LANES), jnp.bfloat16)
-        none24 = jnp.zeros((3 * GROUP, 2 * LANES), jnp.float32)
+        none32 = jnp.zeros((32, 2 * LANES), jnp.bfloat16)
         found = []
         for block in range(tile_width // STEP):
             left_side = [jnp.concatenate([v[block]] * 2, 1) * window for v in near] + [none]
-            means = [jnp.concatenate([a[block]] * 2, 1) * only for a in far for _ in range(3)]
-            left_side.append(jnp.concatenate(means + [none24], 0).astype(jnp.bfloat16))
+            two, last = [jnp.concatenate([a[block]] * 2, 1) * only for a in far]
+            left_side += [two, two, two, last, last, none32]
             reached = slice(block * STEP, block * STEP + span)
             products = jnp.dot(
                 right_side[reached], jnp.concatenate(left_side, 0), preferred_element_type=jnp.float32
@@ -298,7 +304,7 @@
         out_shape=jax.ShapeDtypeStruct((band_rows, tile_width), jnp.float32),
         in_specs=[VMEM, VMEM, VMEM],
         out_specs=VMEM,
-        scratch_shapes=[pltpu.VMEM((lines.shape[0] + 8, TILES, LANES), jnp.float32)],
+        scratch_shapes=[pltpu.VMEM(((lines.shape[0] + 9) * TILES, LANES), jnp.float32)],
         compiler_params=pltpu.CompilerParams(vmem_limit_bytes=16 * 2**20),
     )(lines, start, low)
 

time: 14.8 us -> 14.8 us (level)
  no operation moved by 1% of the time
where the time goes in v8:
time: 14.8 us; the launch traced here: 14.5 us
  blocking collectives  11.3 us (76%)
  Pallas kernels  2.49 us (17%)
  starting transfers between devices  0.51 us (3%)
  waiting for transfers between devices  0.19 us (1%)
    all_to_all x1, blocking collectives, on_device(): lax.all_to_all(pieces, ('rows', 'cols'), split_axis=0, concat_axis=0, til...  11.3 us
    pallas_call x1, Pallas kernels, score(): pl.pallas_call(functools.partial(score_kernel, order), out_shape=jax.Shap...  1.55 us
    pallas_call x1, Pallas kernels, cut_own(): pl.pallas_call(functools.partial(own_kernel, tiles), out_shape=[jax.Shape...  0.84 us
    ppermute x1, starting transfers between devices, on_device(): right_other = lax.ppermute(right_image, 'cols', swap)  0.45 us
  transfers between devices with their start and end apart: 2, of which 1 were waited for; matrix products, arithmetic and copies ran while one was open for 0% of the time, Pallas kernels for 6%

profile of v8, /device:TPU:1, one launch (start us, length us, event | category | flops | bytes accessed | tf_op | source)
XLA Modules:
  0.0 14.5 jit_solution(11823210891442131784)
XLA Ops:
  0.0 0.1 collective-permute-start
  0.1 0.5 %collective-permute-start.1 = (bf16[1,2048]{1,0:T(2,128)(2,1)}, bf16[1,2048]{1,0:T(2,128)(2,1)S(1)}, u32[]{:S(2)}, u32[]{:S(2)}) collective-permute-start(bf16[1,2048]{1,0:T(2,128)(2,1)} %right_hbm.1), channel_id=1, source_target_pairs={{0,1},{1,0},{2,3},{3,2},{4,5},{5,4},{6,7},{7,6},{8,9},{9,8},{10,11... | collective-permute-start | bytes 12296 | tf_op jit(solution)/shard_map/ppermute | solution.py:317
  0.5 0.8 %shard_map.37 = (bf16[4,1,8,128]{3,2,1,0:T(8,128)(2,1)S(1)}, s32[8,128]{1,0:T(8,128)S(1)}, s32[8,128]{1,0:T(8,128)S(1)}) custom-call(bf16[1,2048]{1,0:T(2,128)(2,1)} %left_hbm.1, bf16[1,2048]{1,0:T(2,128)(2,1)} %right_hbm.1, s32[2,8]{1,0:T(2,128)} %bitcast.3), custom_call_target="tpu_custom_call" | custom-call | flops 1000000 | bytes 65536 | tf_op jit(solution)/shard_map/pallas_call | solution.py:97
  1.4 0.0 collective-permute-done.left_ref
  1.4 0.2 %collective-permute-done.1.right_ref = bf16[1,2048]{1,0:T(2,128)(2,1)S(1)} collective-permute-done((bf16[1,2048]{1,0:T(2,128)(2,1)}, bf16[1,2048]{1,0:T(2,128)(2,1)S(1)}, u32[]{:S(2)}, u32[]{:S(2)}) %collective-permute-start.1) | collective-permute-done | bytes 4128 | tf_op jit(solution)/shard_map/ppermute | solution.py:317
  1.6 0.1 shard_map.38
  1.7 11.3 %all_to_all.5 = bf16[16,2,1,8,128]{4,3,2,1,0:T(8,128)(2,1)S(1)} all-to-all(bf16[16,2,1,8,128]{4,3,2,1,0:T(8,128)(2,1)S(1)} %shard_map.38), channel_id=1, replica_groups={{28,10,14,18,22,25,6,2,12,9,20,17,1,26,30,4},{29,11,15,19,23,24,7,3,13,..., dimensions={0} | all-to-all | bytes 131072 | tf_op jit(solution)/shard_map/all_to_all | solution.py:322
  13.0 1.5 %shard_map.39 = f32[8,256]{1,0:T(8,128)} custom-call(bf16[32,8,128]{2,1,0:T(8,128)(2,1)S(1)} %bitcast.2, s32[8,128]{1,0:T(8,128)S(1)} %get-tuple-element.9.start_ref, s32[8,128]{1,0:T(8,128)S(1)} %get-tuple-element.10.low_ref), custom_call_target="tpu_custom_call" | custom-call | tf_op jit(solution)/shard_map/pallas_call | solution.py:302
Async XLA Ops:
  0.0 1.4 %collective-permute-start = (bf16[1,2048]{1,0:T(2,128)(2,1)}, bf16[1,2048]{1,0:T(2,128)(2,1)S(1)}, u32[]{:S(2)}, u32[]{:S(2)}) collective-permute-start(bf16[1,2048]{1,0:T(2,128)(2,1)} %left_hbm.1), channel_id=1, source_target_pairs={{0,1},{1,0},{2,3},{3,2},{4,5},{5,4},{6,7},{7,6},{8,9},{9,8},{10,11... | collective-permute-start | bytes 12296 | tf_op jit(solution)/shard_map/ppermute | solution.py:316
  0.1 1.5 %collective-permute-start.1 = (bf16[1,2048]{1,0:T(2,128)(2,1)}, bf16[1,2048]{1,0:T(2,128)(2,1)S(1)}, u32[]{:S(2)}, u32[]{:S(2)}) collective-permute-start(bf16[1,2048]{1,0:T(2,128)(2,1)} %right_hbm.1), channel_id=1, source_target_pairs={{0,1},{1,0},{2,3},{3,2},{4,5},{5,4},{6,7},{7,6},{8,9},{9,8},{10,11... | collective-permute-start | bytes 12296 | tf_op jit(solution)/shard_map/ppermute | solution.py:317

commit v9 on v8

--- a/solution.py
+++ b/solution.py
@@ -262,16 +262,16 @@
         far_side += [p.astype(jnp.float32) for p in parts(right_scale)] + [jnp.zeros_like(low)]
         far_side = jnp.transpose(jnp.concatenate(far_side, 0).astype(jnp.bfloat16))
         right_side = jnp.concatenate([near_side, far_side], 1)
-        depth = right_side.shape[1]
+        depth = far_side.shape[1]
         near = [spread_out(v, lane_group) for v in shifted_left]
         high, middle, low = [p.astype(jnp.float32) for p in parts(-left_total)]
         far = [jnp.concatenate(p, 0).astype(jnp.bfloat16) for p in ((high, middle), (low, low))]
         far = [spread_out(p, lane_group) for p in far]
         source = lax.broadcasted_iota(jnp.int32, (depth, 2 * LANES), 0)
         owner = lax.broadcasted_iota(jnp.int32, (depth, 2 * LANES), 1) // STEP
-        picked = (source >= 128 + 10 * GROUP) & ((source & 7) == owner)
+        picked = (source >= 10 * GROUP) & ((source & 7) == owner)
         picks = jnp.where(picked, 1.0, 0.0).astype(jnp.bfloat16)
-        scale = jnp.dot(right_side, picks, preferred_element_type=jnp.float32)
+        scale = jnp.dot(far_side, picks, preferred_element_type=jnp.float32)
         none = jnp.zeros((16, 2 * LANES), jnp.bfloat16)
         none32 = jnp.zeros((32, 2 * LANES), jnp.bfloat16)
         found = []

time: 14.8 us -> 14.7 us (level)
  no operation moved by 1% of the time
where the time goes in v9:
time: 14.7 us; the launch traced here: 14.5 us
  blocking collectives  11.3 us (77%)
  Pallas kernels  2.43 us (17%)
  starting transfers between devices  0.51 us (3%)
  waiting for transfers between devices  0.19 us (1%)
    all_to_all x1, blocking collectives, on_device(): lax.all_to_all(pieces, ('rows', 'cols'), split_axis=0, concat_axis=0, til...  11.3 us
    pallas_call x1, Pallas kernels, score(): pl.pallas_call(functools.partial(score_kernel, order), out_shape=jax.Shap...  1.49 us
    pallas_call x1, Pallas kernels, cut_own(): pl.pallas_call(functools.partial(own_kernel, tiles), out_shape=[jax.Shape...  0.84 us
    ppermute x1, starting transfers between devices, on_device(): right_other = lax.ppermute(right_image, 'cols', swap)  0.45 us
  transfers between devices with their start and end apart: 2, of which 1 were waited for; matrix products, arithmetic and copies ran while one was open for 0% of the time, Pallas kernels for 6%

profile of v9, /device:TPU:1, one launch (start us, length us, event | category | flops | bytes accessed | tf_op | source)
XLA Modules:
  0.0 14.5 jit_solution(64961974515895518)
XLA Ops:
  0.0 0.1 collective-permute-start
  0.1 0.5 %collective-permute-start.1 = (bf16[1,2048]{1,0:T(2,128)(2,1)}, bf16[1,2048]{1,0:T(2,128)(2,1)S(1)}, u32[]{:S(2)}, u32[]{:S(2)}) collective-permute-start(bf16[1,2048]{1,0:T(2,128)(2,1)} %right_hbm.1), channel_id=1, source_target_pairs={{0,1},{1,0},{2,3},{3,2},{4,5},{5,4},{6,7},{7,6},{8,9},{9,8},{10,11... | collective-permute-start | bytes 12296 | tf_op jit(solution)/shard_map/ppermute | solution.py:317
  0.5 0.8 %shard_map.37 = (bf16[4,1,8,128]{3,2,1,0:T(8,128)(2,1)S(1)}, s32[8,128]{1,0:T(8,128)S(1)}, s32[8,128]{1,0:T(8,128)S(1)}) custom-call(bf16[1,2048]{1,0:T(2,128)(2,1)} %left_hbm.1, bf16[1,2048]{1,0:T(2,128)(2,1)} %right_hbm.1, s32[2,8]{1,0:T(2,128)} %bitcast.3), custom_call_target="tpu_custom_call" | custom-call | flops 1000000 | bytes 65536 | tf_op jit(solution)/shard_map/pallas_call | solution.py:97
  1.4 0.0 collective-permute-done.left_ref
  1.4 0.2 %collective-permute-done.1.right_ref = bf16[1,2048]{1,0:T(2,128)(2,1)S(1)} collective-permute-done((bf16[1,2048]{1,0:T(2,128)(2,1)}, bf16[1,2048]{1,0:T(2,128)(2,1)S(1)}, u32[]{:S(2)}, u32[]{:S(2)}) %collective-permute-start.1) | collective-permute-done | bytes 4128 | tf_op jit(solution)/shard_map/ppermute | solution.py:317
  1.6 0.1 shard_map.38
  1.7 11.3 %all_to_all.5 = bf16[16,2,1,8,128]{4,3,2,1,0:T(8,128)(2,1)S(1)} all-to-all(bf16[16,2,1,8,128]{4,3,2,1,0:T(8,128)(2,1)S(1)} %shard_map.38), channel_id=1, replica_groups={{28,10,14,18,22,25,6,2,12,9,20,17,1,26,30,4},{29,11,15,19,23,24,7,3,13,..., dimensions={0} | all-to-all | bytes 131072 | tf_op jit(solution)/shard_map/all_to_all | solution.py:322
  13.0 1.5 %shard_map.39 = f32[8,256]{1,0:T(8,128)} custom-call(bf16[32,8,128]{2,1,0:T(8,128)(2,1)S(1)} %bitcast.2, s32[8,128]{1,0:T(8,128)S(1)} %get-tuple-element.9.start_ref, s32[8,128]{1,0:T(8,128)S(1)} %get-tuple-element.10.low_ref), custom_call_target="tpu_custom_call" | custom-call | tf_op jit(solution)/shard_map/pallas_call | solution.py:302
Async XLA Ops:
  0.0 1.4 %collective-permute-start = (bf16[1,2048]{1,0:T(2,128)(2,1)}, bf16[1,2048]{1,0:T(2,128)(2,1)S(1)}, u32[]{:S(2)}, u32[]{:S(2)}) collective-permute-start(bf16[1,2048]{1,0:T(2,128)(2,1)} %left_hbm.1), channel_id=1, source_target_pairs={{0,1},{1,0},{2,3},{3,2},{4,5},{5,4},{6,7},{7,6},{8,9},{9,8},{10,11... | collective-permute-start | bytes 12296 | tf_op jit(solution)/shard_map/ppermute | solution.py:316
  0.1 1.5 %collective-permute-start.1 = (bf16[1,2048]{1,0:T(2,128)(2,1)}, bf16[1,2048]{1,0:T(2,128)(2,1)S(1)}, u32[]{:S(2)}, u32[]{:S(2)}) collective-permute-start(bf16[1,2048]{1,0:T(2,128)(2,1)} %right_hbm.1), channel_id=1, source_target_pairs={{0,1},{1,0},{2,3},{3,2},{4,5},{5,4},{6,7},{7,6},{8,9},{9,8},{10,11... | collective-permute-start | bytes 12296 | tf_op jit(solution)/shard_map/ppermute | solution.py:317

commit v10 on v9

--- a/solution.py
+++ b/solution.py
@@ -68,7 +68,7 @@
             put(pair, line, cut(left_rows, right_rows, LEAD + tile * per_tile))
 
 
-def own_kernel(tiles, left_hbm, right_hbm, ranges_hbm, out_ref, start_ref, low_ref, left_ref, right_ref, ranges_ref, left_rows, right_rows, sems):
+def own_kernel(tiles, left_hbm, right_hbm, ranges_hbm, out_ref, start_ref, cap_ref, masks_ref, picks_ref, left_ref, right_ref, ranges_ref, left_rows, right_rows, sems):
     copies = [
         pltpu.make_async_copy(source, target, sems.at[i])
         for i, (source, target) in enumerate(
@@ -79,11 +79,24 @@
         copy.start()
     left_rows[...] = jnp.zeros_like(left_rows)
     right_rows[...] = jnp.zeros_like(right_rows)
+    row16 = lax.broadcasted_iota(jnp.int32, (16, 2 * LANES), 0)
+    owner16 = lax.broadcasted_iota(jnp.int32, (16, 2 * LANES), 1) // STEP
+    window = jnp.where((row16 >= owner16) & (row16 < owner16 + 7), 1.0, 0.0)
+    masks_ref[0] = window.astype(jnp.bfloat16)
+    masks_ref[1] = jnp.where((row16 & 7) == owner16, 1.0, 0.0).astype(jnp.bfloat16)
+    source = lax.broadcasted_iota(jnp.int32, picks_ref.shape, 0)
+    owner = lax.broadcasted_iota(jnp.int32, picks_ref.shape, 1) // STEP
+    picked = (source >= 10 * GROUP) & ((source & 7) == owner)
+    picks_ref[...] = jnp.where(picked, 1.0, 0.0).astype(jnp.bfloat16)
+    past = lax.broadcasted_iota(jnp.int32, cap_ref.shape, 0) - (
+        lax.broadcasted_iota(jnp.int32, cap_ref.shape, 1) & (STEP - 1)
+    )
     for copy in copies:
         copy.wait()
     tile = lax.axis_index("cols")
     start_ref[...] = jnp.full(start_ref.shape, ranges_ref[0, tile], jnp.int32)
-    low_ref[...] = jnp.full(low_ref.shape, MAXB * DB - DB * ranges_ref[1, tile], jnp.int32)
+    inside = (past >= MAXB * DB - DB * ranges_ref[1, tile]) & (past < MAXB * DB)
+    cap_ref[...] = jnp.where(inside, FAR, -FAR)
 
     def put(pair, line, piece):
         out_ref[pair, line] = piece
@@ -99,10 +112,12 @@
         out_shape=[
             jax.ShapeDtypeStruct((tiles // 2, strip, TILES, LANES), jnp.bfloat16),
             jax.ShapeDtypeStruct((8, LANES), jnp.int32),
-            jax.ShapeDtypeStruct((8, LANES), jnp.int32),
+            jax.ShapeDtypeStruct((MAXB * DB + STEP, LANES), jnp.float32),
+            jax.ShapeDtypeStruct((2, 16, 2 * LANES), jnp.bfloat16),
+            jax.ShapeDtypeStruct((14 * GROUP, 2 * LANES), jnp.bfloat16),
         ],
         in_specs=[HBM, HBM, HBM],
-        out_specs=[VMEM, VMEM, VMEM],
+        out_specs=[VMEM] * 5,
         scratch_shapes=[
             pltpu.VMEM(left.shape, left.dtype),
             pltpu.VMEM(right.shape, right.dtype),
@@ -214,22 +229,14 @@
     return jnp.concatenate(out, 1)
 
 
-def score_kernel(order, lines_ref, start_ref, low_ref, out_ref, rows):
+def score_kernel(order, lines_ref, start_ref, cap_ref, masks_ref, picks_ref, out_ref, rows):
     band_rows, tile_width = out_ref.shape
     reach = tile_width + MAXB * DB
     span = MAXB * DB + STEP
-    row16 = lax.broadcasted_iota(jnp.int32, (16, 2 * LANES), 0)
-    owner16 = lax.broadcasted_iota(jnp.int32, (16, 2 * LANES), 1) // STEP
-    window = jnp.where((row16 >= owner16) & (row16 < owner16 + 7), 1.0, 0.0).astype(jnp.bfloat16)
-    only = jnp.where((row16 & 7) == owner16, 1.0, 0.0).astype(jnp.bfloat16)
+    window, only = masks_ref[0], masks_ref[1]
     lane16 = lax.broadcasted_iota(jnp.int32, (16, LANES), 1) // STEP
     lane_group = [jnp.where(lane16 == p, 1.0, 0.0) for p in range(LANES // STEP)]
     lane_group = [v.astype(jnp.bfloat16) for v in lane_group]
-    past = lax.broadcasted_iota(jnp.int32, (span, LANES), 0) - (
-        lax.broadcasted_iota(jnp.int32, (span, LANES), 1) & (STEP - 1)
-    )
-    inside = (past >= low_ref[0:1, :]) & (past < MAXB * DB)
-    cap = jnp.where(inside, FAR, -FAR)
     always = (DB + STEP, MAXB * DB)
     height = lines_ref.shape[0]
     each = height // len(order)
@@ -262,16 +269,11 @@
         far_side += [p.astype(jnp.float32) for p in parts(right_scale)] + [jnp.zeros_like(low)]
         far_side = jnp.transpose(jnp.concatenate(far_side, 0).astype(jnp.bfloat16))
         right_side = jnp.concatenate([near_side, far_side], 1)
-        depth = far_side.shape[1]
         near = [spread_out(v, lane_group) for v in shifted_left]
         high, middle, low = [p.astype(jnp.float32) for p in parts(-left_total)]
         far = [jnp.concatenate(p, 0).astype(jnp.bfloat16) for p in ((high, middle), (low, low))]
         far = [spread_out(p, lane_group) for p in far]
-        source = lax.broadcasted_iota(jnp.int32, (depth, 2 * LANES), 0)
-        owner = lax.broadcasted_iota(jnp.int32, (depth, 2 * LANES), 1) // STEP
-        picked = (source >= 10 * GROUP) & ((source & 7) == owner)
-        picks = jnp.where(picked, 1.0, 0.0).astype(jnp.bfloat16)
-        scale = jnp.dot(far_side, picks, preferred_element_type=jnp.float32)
+        scale = jnp.dot(far_side, picks_ref[...], preferred_element_type=jnp.float32)
         none = jnp.zeros((16, 2 * LANES), jnp.bfloat16)
         none32 = jnp.zeros((32, 2 * LANES), jnp.bfloat16)
         found = []
@@ -288,9 +290,9 @@
                 at = slice(half * LANES, (half + 1) * LANES)
                 scaled = products[:, at] * scale[reached, at]
                 kept = [
-                    jnp.minimum(scaled[: always[0]], cap[: always[0]]),
+                    jnp.minimum(scaled[: always[0]], cap_ref[: always[0]]),
                     scaled[always[0] : always[1]],
-                    jnp.minimum(scaled[always[1] :], cap[always[1] :]),
+                    jnp.minimum(scaled[always[1] :], cap_ref[always[1] :]),
                 ]
                 halves.append(jnp.max(functools.reduce(jnp.maximum, [fold(v) for v in kept]), axis=0, keepdims=True))
             found.append(jnp.concatenate(halves, 1))
@@ -298,15 +300,15 @@
         out_ref[group * GROUP : (group + 1) * GROUP, :] = jnp.maximum(best, -2.0)
 
 
-def score(lines, start, low, order, band_rows, tile_width):
+def score(lines, constants, order, band_rows, tile_width):
     return pl.pallas_call(
         functools.partial(score_kernel, order),
         out_shape=jax.ShapeDtypeStruct((band_rows, tile_width), jnp.float32),
-        in_specs=[VMEM, VMEM, VMEM],
+        in_specs=[VMEM] * 5,
         out_specs=VMEM,
         scratch_shapes=[pltpu.VMEM(((lines.shape[0] + 9) * TILES, LANES), jnp.float32)],
         compiler_params=pltpu.CompilerParams(vmem_limit_bytes=16 * 2**20),
-    )(lines, start, low)
+    )(lines, *constants)
 
 
 def on_device(left_image, right_image, ranges):
@@ -315,7 +317,7 @@
     swap = [(i, i ^ 1) for i in range(tiles)]
     left_other = lax.ppermute(left_image, "cols", swap)
     right_other = lax.ppermute(right_image, "cols", swap)
-    own, start, low = cut_own(left_image, right_image, ranges, tiles)
+    own, *constants = cut_own(left_image, right_image, ranges, tiles)
     pieces = cut_pair(own, left_other, right_other, bands, tiles)
     order = chip_order(bands, tiles // 2)
     groups = [[2 * chip + (side if chip % (tiles // 2) else 1 - side) for chip in order] for side in range(2)]
@@ -323,7 +325,7 @@
         pieces, ("rows", "cols"), split_axis=0, concat_axis=0, tiled=True, axis_index_groups=groups
     )
     lines = lines.reshape(bands * tiles * strip, TILES, LANES)
-    return score(lines, start, low, order, strip * tiles, width // tiles)
+    return score(lines, constants, order, strip * tiles, width // tiles)
 
 
 def solution(mesh):

time: 14.7 us -> 14.7 us (level)
  no operation moved by 1% of the time
where the time goes in v10:
time: 14.7 us; the launch traced here: 14.5 us
  blocking collectives  11.3 us (77%)
  Pallas kernels  2.45 us (17%)
  starting transfers between devices  0.51 us (3%)
  waiting for transfers between devices  0.19 us (1%)
    all_to_all x1, blocking collectives, on_device(): lax.all_to_all(pieces, ('rows', 'cols'), split_axis=0, concat_axis=0, til...  11.3 us
    pallas_call x1, Pallas kernels, score(): pl.pallas_call(functools.partial(score_kernel, order), out_shape=jax.Shap...  1.51 us
    pallas_call x1, Pallas kernels, cut_own(): pl.pallas_call(functools.partial(own_kernel, tiles), out_shape=[jax.Shape...  0.84 us
    ppermute x1, starting transfers between devices, on_device(): right_other = lax.ppermute(right_image, 'cols', swap)  0.45 us
  transfers between devices with their start and end apart: 2, of which 1 were waited for; matrix products, arithmetic and copies ran while one was open for 0% of the time, Pallas kernels for 6%

profile of v10, /device:TPU:1, one launch (start us, length us, event | category | flops | bytes accessed | tf_op | source)
XLA Modules:
  0.0 14.5 jit_solution(4097392306088412123)
XLA Ops:
  0.0 0.1 collective-permute-start
  0.1 0.5 %collective-permute-start.1 = (bf16[1,2048]{1,0:T(2,128)(2,1)}, bf16[1,2048]{1,0:T(2,128)(2,1)S(1)}, u32[]{:S(2)}, u32[]{:S(2)}) collective-permute-start(bf16[1,2048]{1,0:T(2,128)(2,1)} %right_hbm.1), channel_id=1, source_target_pairs={{0,1},{1,0},{2,3},{3,2},{4,5},{5,4},{6,7},{7,6},{8,9},{9,8},{10,11... | collective-permute-start | bytes 12296 | tf_op jit(solution)/shard_map/ppermute | solution.py:319
  0.5 0.8 %shard_map.37 = (bf16[4,1,8,128]{3,2,1,0:T(8,128)(2,1)S(1)}, s32[8,128]{1,0:T(8,128)S(1)}, f32[288,128]{1,0:T(8,128)S(1)}, bf16[2,16,256]{2,1,0:T(8,128)(2,1)S(1)}, bf16[112,256]{1,0:T(8,128)(2,1)S(1)}) custom-call(bf16[1,2048]{1,0:T(2,128)(2,1)} %left_hbm.1, bf16[1,2048]{1,0:T(2,128)(2,1)} %right_hbm.1, s32[2,8]{1,0:T(2,128)} %bitcast.3), custom_call_target="tpu_custom_call" | custom-call | flops 1000000 | bytes 65536 | tf_op jit(solution)/shard_map/pallas_call | solution.py:110
  1.4 0.0 collective-permute-done.left_ref
  1.4 0.2 %collective-permute-done.1.right_ref = bf16[1,2048]{1,0:T(2,128)(2,1)S(1)} collective-permute-done((bf16[1,2048]{1,0:T(2,128)(2,1)}, bf16[1,2048]{1,0:T(2,128)(2,1)S(1)}, u32[]{:S(2)}, u32[]{:S(2)}) %collective-permute-start.1) | collective-permute-done | bytes 4128 | tf_op jit(solution)/shard_map/ppermute | solution.py:319
  1.6 0.1 shard_map.38
  1.7 11.3 %all_to_all.5 = bf16[16,2,1,8,128]{4,3,2,1,0:T(8,128)(2,1)S(1)} all-to-all(bf16[16,2,1,8,128]{4,3,2,1,0:T(8,128)(2,1)S(1)} %shard_map.38), channel_id=1, replica_groups={{28,10,14,18,22,25,6,2,12,9,20,17,1,26,30,4},{29,11,15,19,23,24,7,3,13,..., dimensions={0} | all-to-all | bytes 131072 | tf_op jit(solution)/shard_map/all_to_all | solution.py:324
  13.0 1.5 %shard_map.39 = f32[8,256]{1,0:T(8,128)} custom-call(bf16[32,8,128]{2,1,0:T(8,128)(2,1)S(1)} %bitcast.2, s32[8,128]{1,0:T(8,128)S(1)} %get-tuple-element.11.start_ref, f32[288,128]{1,0:T(8,128)S(1)} %get-tuple-element.12.cap_ref, bf16[2,16,256]{2,1,0:T(8,128)(2,1)S(1)} %get-tuple-element.13.masks_ref, bf16[112,256]{1,0:T(8,128)(2,1)S(1)} %get-tuple-element.14.picks_ref), custom_call_target="tpu_custom_call" | custom-call | tf_op jit(solution)/shard_map/pallas_call | solution.py:304
Async XLA Ops:
  0.0 1.4 %collective-permute-start = (bf16[1,2048]{1,0:T(2,128)(2,1)}, bf16[1,2048]{1,0:T(2,128)(2,1)S(1)}, u32[]{:S(2)}, u32[]{:S(2)}) collective-permute-start(bf16[1,2048]{1,0:T(2,128)(2,1)} %left_hbm.1), channel_id=1, source_target_pairs={{0,1},{1,0},{2,3},{3,2},{4,5},{5,4},{6,7},{7,6},{8,9},{9,8},{10,11... | collective-permute-start | bytes 12296 | tf_op jit(solution)/shard_map/ppermute | solution.py:318
  0.1 1.5 %collective-permute-start.1 = (bf16[1,2048]{1,0:T(2,128)(2,1)}, bf16[1,2048]{1,0:T(2,128)(2,1)S(1)}, u32[]{:S(2)}, u32[]{:S(2)}) collective-permute-start(bf16[1,2048]{1,0:T(2,128)(2,1)} %right_hbm.1), channel_id=1, source_target_pairs={{0,1},{1,0},{2,3},{3,2},{4,5},{5,4},{6,7},{7,6},{8,9},{9,8},{10,11... | collective-permute-start | bytes 12296 | tf_op jit(solution)/shard_map/ppermute | solution.py:319

commit v11 on v10

--- a/solution.py
+++ b/solution.py
@@ -252,7 +252,7 @@
     def moved(pieces, by):
         turned = [pltpu.roll(v, by, 1) for v in pieces]
         ahead_by = [jnp.where(lane < by, a, b) for a, b in zip(turned, turned[1:])]
-        return jnp.concatenate(ahead_by, 1).astype(jnp.bfloat16)
+        return jnp.concatenate(ahead_by, 1)
 
     for group in range(band_rows // GROUP):
         first = (lax.axis_index("rows") * band_rows + group * GROUP) * TILES
@@ -261,7 +261,7 @@
         shifted_right = [moved(tiles[LEFT_TILES:], RIGHT_LEAD - 4 - j + start) for j in range(7)]
         shifted_left = [ahead(left, j, 1)[:, :tile_width] for j in range(7)]
         blank = jnp.zeros((16, reach), jnp.bfloat16)
-        near_side = jnp.transpose(jnp.concatenate(shifted_right + [blank], 0))
+        near_side = jnp.transpose(jnp.concatenate([v.astype(jnp.bfloat16) for v in shifted_right] + [blank], 0))
         _, right_mean, right_scale = moments(shifted_right)
         left_total, _, left_scale = moments(shifted_left)
         high, middle, low = [p.astype(jnp.float32) for p in parts(right_mean)]

time: 14.7 us -> 14.7 us (level)
  no operation moved by 1% of the time
where the time goes in v11:
time: 14.7 us; the launch traced here: 14.5 us
  blocking collectives  11.3 us (77%)
  Pallas kernels  2.47 us (17%)
  starting transfers between devices  0.51 us (3%)
  waiting for transfers between devices  0.19 us (1%)
    all_to_all x1, blocking collectives, on_device(): lax.all_to_all(pieces, ('rows', 'cols'), split_axis=0, concat_axis=0, til...  11.3 us
    pallas_call x1, Pallas kernels, score(): pl.pallas_call(functools.partial(score_kernel, order), out_shape=jax.Shap...  1.53 us
    pallas_call x1, Pallas kernels, cut_own(): pl.pallas_call(functools.partial(own_kernel, tiles), out_shape=[jax.Shape...  0.84 us
    ppermute x1, starting transfers between devices, on_device(): right_other = lax.ppermute(right_image, 'cols', swap)  0.45 us
  transfers between devices with their start and end apart: 2, of which 1 were waited for; matrix products, arithmetic and copies ran while one was open for 0% of the time, Pallas kernels for 6%

profile of v11, /device:TPU:1, one launch (start us, length us, event | category | flops | bytes accessed | tf_op | source)
XLA Modules:
  0.0 14.5 jit_solution(10280401829797014910)
XLA Ops:
  0.0 0.1 collective-permute-start
  0.1 0.5 %collective-permute-start.1 = (bf16[1,2048]{1,0:T(2,128)(2,1)}, bf16[1,2048]{1,0:T(2,128)(2,1)S(1)}, u32[]{:S(2)}, u32[]{:S(2)}) collective-permute-start(bf16[1,2048]{1,0:T(2,128)(2,1)} %right_hbm.1), channel_id=1, source_target_pairs={{0,1},{1,0},{2,3},{3,2},{4,5},{5,4},{6,7},{7,6},{8,9},{9,8},{10,11... | collective-permute-start | bytes 12296 | tf_op jit(solution)/shard_map/ppermute | solution.py:319
  0.5 0.8 %shard_map.37 = (bf16[4,1,8,128]{3,2,1,0:T(8,128)(2,1)S(1)}, s32[8,128]{1,0:T(8,128)S(1)}, f32[288,128]{1,0:T(8,128)S(1)}, bf16[2,16,256]{2,1,0:T(8,128)(2,1)S(1)}, bf16[112,256]{1,0:T(8,128)(2,1)S(1)}) custom-call(bf16[1,2048]{1,0:T(2,128)(2,1)} %left_hbm.1, bf16[1,2048]{1,0:T(2,128)(2,1)} %right_hbm.1, s32[2,8]{1,0:T(2,128)} %bitcast.3), custom_call_target="tpu_custom_call" | custom-call | flops 1000000 | bytes 65536 | tf_op jit(solution)/shard_map/pallas_call | solution.py:110
  1.4 0.0 collective-permute-done.left_ref
  1.4 0.2 %collective-permute-done.1.right_ref = bf16[1,2048]{1,0:T(2,128)(2,1)S(1)} collective-permute-done((bf16[1,2048]{1,0:T(2,128)(2,1)}, bf16[1,2048]{1,0:T(2,128)(2,1)S(1)}, u32[]{:S(2)}, u32[]{:S(2)}) %collective-permute-start.1) | collective-permute-done | bytes 4128 | tf_op jit(solution)/shard_map/ppermute | solution.py:319
  1.6 0.1 shard_map.38
  1.7 11.3 %all_to_all.5 = bf16[16,2,1,8,128]{4,3,2,1,0:T(8,128)(2,1)S(1)} all-to-all(bf16[16,2,1,8,128]{4,3,2,1,0:T(8,128)(2,1)S(1)} %shard_map.38), channel_id=1, replica_groups={{28,10,14,18,22,25,6,2,12,9,20,17,1,26,30,4},{29,11,15,19,23,24,7,3,13,..., dimensions={0} | all-to-all | bytes 131072 | tf_op jit(solution)/shard_map/all_to_all | solution.py:324
  13.0 1.5 %shard_map.39 = f32[8,256]{1,0:T(8,128)} custom-call(bf16[32,8,128]{2,1,0:T(8,128)(2,1)S(1)} %bitcast.2, s32[8,128]{1,0:T(8,128)S(1)} %get-tuple-element.11.start_ref, f32[288,128]{1,0:T(8,128)S(1)} %get-tuple-element.12.cap_ref, bf16[2,16,256]{2,1,0:T(8,128)(2,1)S(1)} %get-tuple-element.13.masks_ref, bf16[112,256]{1,0:T(8,128)(2,1)S(1)} %get-tuple-element.14.picks_ref), custom_call_target="tpu_custom_call" | custom-call | tf_op jit(solution)/shard_map/pallas_call | solution.py:304
Async XLA Ops:
  0.0 1.4 %collective-permute-start = (bf16[1,2048]{1,0:T(2,128)(2,1)}, bf16[1,2048]{1,0:T(2,128)(2,1)S(1)}, u32[]{:S(2)}, u32[]{:S(2)}) collective-permute-start(bf16[1,2048]{1,0:T(2,128)(2,1)} %left_hbm.1), channel_id=1, source_target_pairs={{0,1},{1,0},{2,3},{3,2},{4,5},{5,4},{6,7},{7,6},{8,9},{9,8},{10,11... | collective-permute-start | bytes 12296 | tf_op jit(solution)/shard_map/ppermute | solution.py:318
  0.1 1.5 %collective-permute-start.1 = (bf16[1,2048]{1,0:T(2,128)(2,1)}, bf16[1,2048]{1,0:T(2,128)(2,1)S(1)}, u32[]{:S(2)}, u32[]{:S(2)}) collective-permute-start(bf16[1,2048]{1,0:T(2,128)(2,1)} %right_hbm.1), channel_id=1, source_target_pairs={{0,1},{1,0},{2,3},{3,2},{4,5},{5,4},{6,7},{7,6},{8,9},{9,8},{10,11... | collective-permute-start | bytes 12296 | tf_op jit(solution)/shard_map/ppermute | solution.py:319

commit v12 on v11

--- a/solution.py
+++ b/solution.py
@@ -233,6 +233,7 @@
     band_rows, tile_width = out_ref.shape
     reach = tile_width + MAXB * DB
     span = MAXB * DB + STEP
+    start = start_ref[0, 0]
     window, only = masks_ref[0], masks_ref[1]
     lane16 = lax.broadcasted_iota(jnp.int32, (16, LANES), 1) // STEP
     lane_group = [jnp.where(lane16 == p, 1.0, 0.0) for p in range(LANES // STEP)]
@@ -246,7 +247,6 @@
         for line in range(each):
             at = (3 + chip * each + line) * TILES
             rows[at : at + TILES] = lines_ref[member * each + line].astype(jnp.float32)
-    start = start_ref[0, 0]
     lane = lax.broadcasted_iota(jnp.int32, (16, LANES), 1)
 
     def moved(pieces, by):

time: 14.7 us -> 14.7 us (level)
  no operation moved by 1% of the time
where the time goes in v12:
time: 14.7 us; the launch traced here: 14.5 us
  blocking collectives  11.3 us (77%)
  Pallas kernels  2.48 us (17%)
  starting transfers between devices  0.51 us (3%)
  waiting for transfers between devices  0.19 us (1%)
    all_to_all x1, blocking collectives, on_device(): lax.all_to_all(pieces, ('rows', 'cols'), split_axis=0, concat_axis=0, til...  11.3 us
    pallas_call x1, Pallas kernels, score(): pl.pallas_call(functools.partial(score_kernel, order), out_shape=jax.Shap...  1.54 us
    pallas_call x1, Pallas kernels, cut_own(): pl.pallas_call(functools.partial(own_kernel, tiles), out_shape=[jax.Shape...  0.84 us
    ppermute x1, starting transfers between devices, on_device(): right_other = lax.ppermute(right_image, 'cols', swap)  0.45 us
  transfers between devices with their start and end apart: 2, of which 1 were waited for; matrix products, arithmetic and copies ran while one was open for 0% of the time, Pallas kernels for 6%

profile of v12, /device:TPU:1, one launch (start us, length us, event | category | flops | bytes accessed | tf_op | source)
XLA Modules:
  0.0 14.5 jit_solution(11101000393435450816)
XLA Ops:
  0.0 0.1 collective-permute-start
  0.1 0.5 %collective-permute-start.1 = (bf16[1,2048]{1,0:T(2,128)(2,1)}, bf16[1,2048]{1,0:T(2,128)(2,1)S(1)}, u32[]{:S(2)}, u32[]{:S(2)}) collective-permute-start(bf16[1,2048]{1,0:T(2,128)(2,1)} %right_hbm.1), channel_id=1, source_target_pairs={{0,1},{1,0},{2,3},{3,2},{4,5},{5,4},{6,7},{7,6},{8,9},{9,8},{10,11... | collective-permute-start | bytes 12296 | tf_op jit(solution)/shard_map/ppermute | solution.py:319
  0.5 0.8 %shard_map.37 = (bf16[4,1,8,128]{3,2,1,0:T(8,128)(2,1)S(1)}, s32[8,128]{1,0:T(8,128)S(1)}, f32[288,128]{1,0:T(8,128)S(1)}, bf16[2,16,256]{2,1,0:T(8,128)(2,1)S(1)}, bf16[112,256]{1,0:T(8,128)(2,1)S(1)}) custom-call(bf16[1,2048]{1,0:T(2,128)(2,1)} %left_hbm.1, bf16[1,2048]{1,0:T(2,128)(2,1)} %right_hbm.1, s32[2,8]{1,0:T(2,128)} %bitcast.3), custom_call_target="tpu_custom_call" | custom-call | flops 1000000 | bytes 65536 | tf_op jit(solution)/shard_map/pallas_call | solution.py:110
  1.4 0.0 collective-permute-done.left_ref
  1.4 0.2 %collective-permute-done.1.right_ref = bf16[1,2048]{1,0:T(2,128)(2,1)S(1)} collective-permute-done((bf16[1,2048]{1,0:T(2,128)(2,1)}, bf16[1,2048]{1,0:T(2,128)(2,1)S(1)}, u32[]{:S(2)}, u32[]{:S(2)}) %collective-permute-start.1) | collective-permute-done | bytes 4128 | tf_op jit(solution)/shard_map/ppermute | solution.py:319
  1.6 0.1 shard_map.38
  1.7 11.3 %all_to_all.5 = bf16[16,2,1,8,128]{4,3,2,1,0:T(8,128)(2,1)S(1)} all-to-all(bf16[16,2,1,8,128]{4,3,2,1,0:T(8,128)(2,1)S(1)} %shard_map.38), channel_id=1, replica_groups={{28,10,14,18,22,25,6,2,12,9,20,17,1,26,30,4},{29,11,15,19,23,24,7,3,13,..., dimensions={0} | all-to-all | bytes 131072 | tf_op jit(solution)/shard_map/all_to_all | solution.py:324
  13.0 1.5 %shard_map.39 = f32[8,256]{1,0:T(8,128)} custom-call(bf16[32,8,128]{2,1,0:T(8,128)(2,1)S(1)} %bitcast.2, s32[8,128]{1,0:T(8,128)S(1)} %get-tuple-element.11.start_ref, f32[288,128]{1,0:T(8,128)S(1)} %get-tuple-element.12.cap_ref, bf16[2,16,256]{2,1,0:T(8,128)(2,1)S(1)} %get-tuple-element.13.masks_ref, bf16[112,256]{1,0:T(8,128)(2,1)S(1)} %get-tuple-element.14.picks_ref), custom_call_target="tpu_custom_call" | custom-call | tf_op jit(solution)/shard_map/pallas_call | solution.py:304
Async XLA Ops:
  0.0 1.4 %collective-permute-start = (bf16[1,2048]{1,0:T(2,128)(2,1)}, bf16[1,2048]{1,0:T(2,128)(2,1)S(1)}, u32[]{:S(2)}, u32[]{:S(2)}) collective-permute-start(bf16[1,2048]{1,0:T(2,128)(2,1)} %left_hbm.1), channel_id=1, source_target_pairs={{0,1},{1,0},{2,3},{3,2},{4,5},{5,4},{6,7},{7,6},{8,9},{9,8},{10,11... | collective-permute-start | bytes 12296 | tf_op jit(solution)/shard_map/ppermute | solution.py:318
  0.1 1.5 %collective-permute-start.1 = (bf16[1,2048]{1,0:T(2,128)(2,1)}, bf16[1,2048]{1,0:T(2,128)(2,1)S(1)}, u32[]{:S(2)}, u32[]{:S(2)}) collective-permute-start(bf16[1,2048]{1,0:T(2,128)(2,1)} %right_hbm.1), channel_id=1, source_target_pairs={{0,1},{1,0},{2,3},{3,2},{4,5},{5,4},{6,7},{7,6},{8,9},{9,8},{10,11... | collective-permute-start | bytes 12296 | tf_op jit(solution)/shard_map/ppermute | solution.py:319

commit v13 on v11

--- a/solution.py
+++ b/solution.py
@@ -139,10 +139,11 @@
 
     def put(pair, line, piece):
         mine = own_ref[pair, line]
+        lines = [jnp.where(core == 0, mine, piece), jnp.where(core == 0, piece, mine)]
         for band in range(bands):
             member = order.index(band * (tiles // 2) + pair)
-            out_ref[member, core, line] = mine
-            out_ref[member, 1 - core, line] = piece
+            for row in range(2):
+                out_ref[member, row, line] = lines[row]
 
     cut_all(tiles, left_ref, right_ref, left_rows, right_rows, put)
 

time: 14.7 us -> 14.7 us (level)
  no operation moved by 1% of the time
where the time goes in v13:
time: 14.7 us; the launch traced here: 14.5 us
  blocking collectives  11.3 us (77%)
  Pallas kernels  2.47 us (17%)
  starting transfers between devices  0.51 us (3%)
  waiting for transfers between devices  0.19 us (1%)
    all_to_all x1, blocking collectives, on_device(): lax.all_to_all(pieces, ('rows', 'cols'), split_axis=0, concat_axis=0, til...  11.3 us
    pallas_call x1, Pallas kernels, score(): pl.pallas_call(functools.partial(score_kernel, order), out_shape=jax.Shap...  1.53 us
    pallas_call x1, Pallas kernels, cut_own(): pl.pallas_call(functools.partial(own_kernel, tiles), out_shape=[jax.Shape...  0.84 us
    ppermute x1, starting transfers between devices, on_device(): right_other = lax.ppermute(right_image, 'cols', swap)  0.45 us
  transfers between devices with their start and end apart: 2, of which 1 were waited for; matrix products, arithmetic and copies ran while one was open for 0% of the time, Pallas kernels for 6%

profile of v13, /device:TPU:1, one launch (start us, length us, event | category | flops | bytes accessed | tf_op | source)
XLA Modules:
  0.0 14.5 jit_solution(1379785745394717958)
XLA Ops:
  0.0 0.1 collective-permute-start
  0.1 0.5 %collective-permute-start.1 = (bf16[1,2048]{1,0:T(2,128)(2,1)}, bf16[1,2048]{1,0:T(2,128)(2,1)S(1)}, u32[]{:S(2)}, u32[]{:S(2)}) collective-permute-start(bf16[1,2048]{1,0:T(2,128)(2,1)} %right_hbm.1), channel_id=1, source_target_pairs={{0,1},{1,0},{2,3},{3,2},{4,5},{5,4},{6,7},{7,6},{8,9},{9,8},{10,11... | collective-permute-start | bytes 12296 | tf_op jit(solution)/shard_map/ppermute | solution.py:320
  0.5 0.8 %shard_map.37 = (bf16[4,1,8,128]{3,2,1,0:T(8,128)(2,1)S(1)}, s32[8,128]{1,0:T(8,128)S(1)}, f32[288,128]{1,0:T(8,128)S(1)}, bf16[2,16,256]{2,1,0:T(8,128)(2,1)S(1)}, bf16[112,256]{1,0:T(8,128)(2,1)S(1)}) custom-call(bf16[1,2048]{1,0:T(2,128)(2,1)} %left_hbm.1, bf16[1,2048]{1,0:T(2,128)(2,1)} %right_hbm.1, s32[2,8]{1,0:T(2,128)} %bitcast.3), custom_call_target="tpu_custom_call" | custom-call | flops 1000000 | bytes 65536 | tf_op jit(solution)/shard_map/pallas_call | solution.py:110
  1.4 0.0 collective-permute-done.left_ref
  1.4 0.2 %collective-permute-done.1.right_ref = bf16[1,2048]{1,0:T(2,128)(2,1)S(1)} collective-permute-done((bf16[1,2048]{1,0:T(2,128)(2,1)}, bf16[1,2048]{1,0:T(2,128)(2,1)S(1)}, u32[]{:S(2)}, u32[]{:S(2)}) %collective-permute-start.1) | collective-permute-done | bytes 4128 | tf_op jit(solution)/shard_map/ppermute | solution.py:320
  1.6 0.1 shard_map.38
  1.7 11.3 %all_to_all.5 = bf16[16,2,1,8,128]{4,3,2,1,0:T(8,128)(2,1)S(1)} all-to-all(bf16[16,2,1,8,128]{4,3,2,1,0:T(8,128)(2,1)S(1)} %shard_map.38), channel_id=1, replica_groups={{28,10,14,18,22,25,6,2,12,9,20,17,1,26,30,4},{29,11,15,19,23,24,7,3,13,..., dimensions={0} | all-to-all | bytes 131072 | tf_op jit(solution)/shard_map/all_to_all | solution.py:325
  13.0 1.5 %shard_map.39 = f32[8,256]{1,0:T(8,128)} custom-call(bf16[32,8,128]{2,1,0:T(8,128)(2,1)S(1)} %bitcast.2, s32[8,128]{1,0:T(8,128)S(1)} %get-tuple-element.11.start_ref, f32[288,128]{1,0:T(8,128)S(1)} %get-tuple-element.12.cap_ref, bf16[2,16,256]{2,1,0:T(8,128)(2,1)S(1)} %get-tuple-element.13.masks_ref, bf16[112,256]{1,0:T(8,128)(2,1)S(1)} %get-tuple-element.14.picks_ref), custom_call_target="tpu_custom_call" | custom-call | tf_op jit(solution)/shard_map/pallas_call | solution.py:305
Async XLA Ops:
  0.0 1.4 %collective-permute-start = (bf16[1,2048]{1,0:T(2,128)(2,1)}, bf16[1,2048]{1,0:T(2,128)(2,1)S(1)}, u32[]{:S(2)}, u32[]{:S(2)}) collective-permute-start(bf16[1,2048]{1,0:T(2,128)(2,1)} %left_hbm.1), channel_id=1, source_target_pairs={{0,1},{1,0},{2,3},{3,2},{4,5},{5,4},{6,7},{7,6},{8,9},{9,8},{10,11... | collective-permute-start | bytes 12296 | tf_op jit(solution)/shard_map/ppermute | solution.py:319
  0.1 1.5 %collective-permute-start.1 = (bf16[1,2048]{1,0:T(2,128)(2,1)}, bf16[1,2048]{1,0:T(2,128)(2,1)S(1)}, u32[]{:S(2)}, u32[]{:S(2)}) collective-permute-start(bf16[1,2048]{1,0:T(2,128)(2,1)} %right_hbm.1), channel_id=1, source_target_pairs={{0,1},{1,0},{2,3},{3,2},{4,5},{5,4},{6,7},{7,6},{8,9},{9,8},{10,11... | collective-permute-start | bytes 12296 | tf_op jit(solution)/shard_map/ppermute | solution.py:320

commit v14 on v11

--- a/solution.py
+++ b/solution.py
@@ -189,8 +189,11 @@
     return [high, middle, low]
 
 
-def sum_of(values):
-    return functools.reduce(lambda a, b: a + b, values)
+def tree_sum(values):
+    while len(values) > 1:
+        pairs = [a + b for a, b in zip(values[::2], values[1::2])]
+        values = pairs + values[len(pairs) * 2 :]
+    return values[0]
 
 
 def fold(values):
@@ -217,15 +220,15 @@
     halves = [found[:, h * LANES : (h + 1) * LANES] for h in range(2)]
     out = []
     for to in range(2):
-        result = jnp.zeros((GROUP, LANES), jnp.float32)
+        terms = []
         for half in range(2):
             for k in range(groups):
                 turned = halves[half] if k == 0 else pltpu.roll(halves[half], STEP * k, 1)
                 for up in sorted({(half - to) * groups - k, (half - to) * groups + (groups - k if k else 0)}):
                     chosen = (row // groups == half) & (row - (to * groups + lane) == up)
                     by = up % GROUP
-                    result = jnp.where(chosen, pltpu.roll(turned, by, 0) if by else turned, result)
-        out.append(result)
+                    terms.append(jnp.where(chosen, pltpu.roll(turned, by, 0) if by else turned, 0.0))
+        out.append(tree_sum(terms))
     return jnp.concatenate(out, 1)
 
 

time: 14.7 us -> 14.7 us (level)
  no operation moved by 1% of the time
where the time goes in v14:
time: 14.7 us; the launch traced here: 14.5 us
  blocking collectives  11.3 us (77%)
  Pallas kernels  2.47 us (17%)
  starting transfers between devices  0.51 us (3%)
  waiting for transfers between devices  0.19 us (1%)
    all_to_all x1, blocking collectives, on_device(): lax.all_to_all(pieces, ('rows', 'cols'), split_axis=0, concat_axis=0, til...  11.3 us
    pallas_call x1, Pallas kernels, score(): pl.pallas_call(functools.partial(score_kernel, order), out_shape=jax.Shap...  1.53 us
    pallas_call x1, Pallas kernels, cut_own(): pl.pallas_call(functools.partial(own_kernel, tiles), out_shape=[jax.Shape...  0.84 us
    ppermute x1, starting transfers between devices, on_device(): right_other = lax.ppermute(right_image, 'cols', swap)  0.45 us
  transfers between devices with their start and end apart: 2, of which 1 were waited for; matrix products, arithmetic and copies ran while one was open for 0% of the time, Pallas kernels for 6%

profile of v14, /device:TPU:1, one launch (start us, length us, event | category | flops | bytes accessed | tf_op | source)
XLA Modules:
  0.0 14.5 jit_solution(13852164148563854463)
XLA Ops:
  0.0 0.1 collective-permute-start
  0.1 0.5 %collective-permute-start.1 = (bf16[1,2048]{1,0:T(2,128)(2,1)}, bf16[1,2048]{1,0:T(2,128)(2,1)S(1)}, u32[]{:S(2)}, u32[]{:S(2)}) collective-permute-start(bf16[1,2048]{1,0:T(2,128)(2,1)} %right_hbm.1), channel_id=1, source_target_pairs={{0,1},{1,0},{2,3},{3,2},{4,5},{5,4},{6,7},{7,6},{8,9},{9,8},{10,11... | collective-permute-start | bytes 12296 | tf_op jit(solution)/shard_map/ppermute | solution.py:322
  0.5 0.8 %shard_map.37 = (bf16[4,1,8,128]{3,2,1,0:T(8,128)(2,1)S(1)}, s32[8,128]{1,0:T(8,128)S(1)}, f32[288,128]{1,0:T(8,128)S(1)}, bf16[2,16,256]{2,1,0:T(8,128)(2,1)S(1)}, bf16[112,256]{1,0:T(8,128)(2,1)S(1)}) custom-call(bf16[1,2048]{1,0:T(2,128)(2,1)} %left_hbm.1, bf16[1,2048]{1,0:T(2,128)(2,1)} %right_hbm.1, s32[2,8]{1,0:T(2,128)} %bitcast.3), custom_call_target="tpu_custom_call" | custom-call | flops 1000000 | bytes 65536 | tf_op jit(solution)/shard_map/pallas_call | solution.py:110
  1.4 0.0 collective-permute-done.left_ref
  1.4 0.2 %collective-permute-done.1.right_ref = bf16[1,2048]{1,0:T(2,128)(2,1)S(1)} collective-permute-done((bf16[1,2048]{1,0:T(2,128)(2,1)}, bf16[1,2048]{1,0:T(2,128)(2,1)S(1)}, u32[]{:S(2)}, u32[]{:S(2)}) %collective-permute-start.1) | collective-permute-done | bytes 4128 | tf_op jit(solution)/shard_map/ppermute | solution.py:322
  1.6 0.1 shard_map.38
  1.7 11.3 %all_to_all.5 = bf16[16,2,1,8,128]{4,3,2,1,0:T(8,128)(2,1)S(1)} all-to-all(bf16[16,2,1,8,128]{4,3,2,1,0:T(8,128)(2,1)S(1)} %shard_map.38), channel_id=1, replica_groups={{28,10,14,18,22,25,6,2,12,9,20,17,1,26,30,4},{29,11,15,19,23,24,7,3,13,..., dimensions={0} | all-to-all | bytes 131072 | tf_op jit(solution)/shard_map/all_to_all | solution.py:327
  13.0 1.5 %shard_map.39 = f32[8,256]{1,0:T(8,128)} custom-call(bf16[32,8,128]{2,1,0:T(8,128)(2,1)S(1)} %bitcast.2, s32[8,128]{1,0:T(8,128)S(1)} %get-tuple-element.11.start_ref, f32[288,128]{1,0:T(8,128)S(1)} %get-tuple-element.12.cap_ref, bf16[2,16,256]{2,1,0:T(8,128)(2,1)S(1)} %get-tuple-element.13.masks_ref, bf16[112,256]{1,0:T(8,128)(2,1)S(1)} %get-tuple-element.14.picks_ref), custom_call_target="tpu_custom_call" | custom-call | tf_op jit(solution)/shard_map/pallas_call | solution.py:307
Async XLA Ops:
  0.0 1.4 %collective-permute-start = (bf16[1,2048]{1,0:T(2,128)(2,1)}, bf16[1,2048]{1,0:T(2,128)(2,1)S(1)}, u32[]{:S(2)}, u32[]{:S(2)}) collective-permute-start(bf16[1,2048]{1,0:T(2,128)(2,1)} %left_hbm.1), channel_id=1, source_target_pairs={{0,1},{1,0},{2,3},{3,2},{4,5},{5,4},{6,7},{7,6},{8,9},{9,8},{10,11... | collective-permute-start | bytes 12296 | tf_op jit(solution)/shard_map/ppermute | solution.py:321
  0.1 1.5 %collective-permute-start.1 = (bf16[1,2048]{1,0:T(2,128)(2,1)}, bf16[1,2048]{1,0:T(2,128)(2,1)S(1)}, u32[]{:S(2)}, u32[]{:S(2)}) collective-permute-start(bf16[1,2048]{1,0:T(2,128)(2,1)} %right_hbm.1), channel_id=1, source_target_pairs={{0,1},{1,0},{2,3},{3,2},{4,5},{5,4},{6,7},{7,6},{8,9},{9,8},{10,11... | collective-permute-start | bytes 12296 | tf_op jit(solution)/shard_map/ppermute | solution.py:322
